TPU v7x, 32 devices: a whole 2x2x4 slice. The times are simulated.
32 devices in a mesh: dp: 8 (over z, y), grp: 4 (over x, core).
Axes of the slice: x: 2, y: 2, z: 4, core: 2. Of those that a mesh axis runs over, the one named last changes fastest.
Arguments:
- image_global: bfloat16 [128, 14, 14, 1024], P(('dp', 'grp')), may hold values from -50 to 50
- image_local: bfloat16 [512, 6, 6, 1024], P(('dp', 'grp')), may hold values from -50 to 50
- w_reduce: bfloat16 [1024, 512], replicated, may hold values from -0.1875 to 0.1875
- w_spatial: bfloat16 [4608, 512], replicated, may hold values from -0.09375 to 0.09375
- w_expand: bfloat16 [512, 2048], replicated, may hold values from -0.25 to 0.25
- w_short: bfloat16 [1024, 2048], replicated, may hold values from -0.1875 to 0.1875
- w_reduce2: bfloat16 [2048, 512], replicated, may hold values from -0.125 to 0.125
- w_spatial2: bfloat16 [4608, 512], replicated, may hold values from -0.09375 to 0.09375
- w_expand2: bfloat16 [512, 2048], replicated, may hold values from -0.25 to 0.25
- gain_mid: float32 [4, 512], replicated, may hold values from 0.25 to 1.75
- shift_mid: float32 [4, 512], replicated, may hold values from -3 to 3
- gain_wide: float32 [3, 2048], replicated, may hold values from 0.25 to 1.75
- shift_wide: float32 [3, 2048], replicated, may hold values from -3 to 3
- cotangent_global: bfloat16 [128, 7, 7, 2048], P(('dp', 'grp')), may hold values from -6 to 6
- cotangent_local: bfloat16 [512, 3, 3, 2048], P(('dp', 'grp')), may hold values from -6 to 6
Outputs:
- output_global: bfloat16 [128, 7, 7, 2048], P(('dp', 'grp'))
- output_local: bfloat16 [512, 3, 3, 2048], P(('dp', 'grp'))
- grad_image_global: bfloat16 [128, 14, 14, 1024], P(('dp', 'grp'))
- grad_image_local: bfloat16 [512, 6, 6, 1024], P(('dp', 'grp'))
- grad_w_reduce: float32 [1024, 512], P('dp')
- grad_w_spatial: float32 [4608, 512], P('dp')
- grad_w_expand: float32 [512, 2048], P('dp')
- grad_w_short: float32 [1024, 2048], P('dp')
- grad_w_reduce2: float32 [2048, 512], P('dp')
- grad_w_spatial2: float32 [4608, 512], P('dp')
- grad_w_expand2: float32 [512, 2048], P('dp')
- grad_gain_mid: float32 [4, 512], replicated
- grad_shift_mid: float32 [4, 512], replicated
- grad_gain_wide: float32 [3, 2048], replicated
- grad_shift_wide: float32 [3, 2048], replicated
All inputs are finite; a program needn't handle non-finite values.
Results may differ from a plain program's by a relative error of at most 0.018.
Values sent between devices are 32-bit elements; how exact they have to be, the bound alone decides.
A program may use at most 192 MiB of HBM per device.

v0:
```python
import jax
import jax.numpy as jnp
from jax import lax
from jax.sharding import PartitionSpec as P

EPS = 1e-05


def gelu(value):
    return jax.nn.gelu(value, approximate=True)


def gelu_back(before, grad):
    return jax.vjp(gelu, before)[1](grad)[0]


def mix(value, weight):
    return jnp.einsum("nhwc,cd->nhwd", value, weight, preferred_element_type=jnp.float32)


def mix_back(grad, weight):
    return jnp.einsum("nhwd,cd->nhwc", grad, weight, preferred_element_type=jnp.float32)


def weight_term(values, grads):
    total = None
    for value, grad in zip(values, grads):
        term = jnp.einsum("nhwc,nhwd->cd", value, grad, preferred_element_type=jnp.float32)
        total = term if total is None else total + term
    return total


def patches(value, stride):
    padded = jnp.pad(value, ((0, 0), (1, 1), (1, 1), (0, 0)))
    extent = value.shape[1] // stride
    reach = stride * (extent - 1) + 1
    taps = []
    for row_tap in range(3):
        for col_tap in range(3):
            taps.append(
                padded[:, row_tap : row_tap + reach : stride, col_tap : col_tap + reach : stride, :]
            )
    return jnp.concatenate(taps, axis=3)


def unpatch(grad, shape, stride):
    width = shape[3]
    extent = grad.shape[1]
    reach = stride * (extent - 1) + 1
    total = jnp.zeros((shape[0], shape[1] + 2, shape[2] + 2, width), jnp.float32)
    for row_tap in range(3):
        for col_tap in range(3):
            number = 3 * row_tap + col_tap
            total = total.at[
                :, row_tap : row_tap + reach : stride, col_tap : col_tap + reach : stride, :
            ].add(grad[..., number * width : (number + 1) * width])
    return total[:, 1:-1, 1:-1, :]


def local_moments(pairs, group):
    first = jnp.concatenate([jnp.sum(pair[group], axis=(0, 1, 2)) for pair in pairs])
    second = jnp.concatenate([jnp.sum(pair[group] * pair[group], axis=(0, 1, 2)) for pair in pairs])
    return (first, second)


def moment_list(sums, pairs):
    devices = lax.axis_size(("dp", "grp"))
    result = []
    start = 0
    for pair in pairs:
        width = pair[0].shape[3]
        moments = []
        for group in range(2):
            count = pair[group].shape[0] * pair[group].shape[1] * pair[group].shape[2] * devices
            mean = sums[2 * group][start : start + width] / count
            spread = sums[2 * group + 1][start : start + width] / count - mean * mean
            moments.append((mean, lax.rsqrt(spread + EPS)))
        result.append(moments)
        start = start + width
    return result


def fresh_moments(pairs):
    global_sum, global_square = local_moments(pairs, 0)
    local_sum, local_square = local_moments(pairs, 1)
    sums = lax.psum((global_sum, global_square, local_sum, local_square), ("dp", "grp"))
    return moment_list(sums, pairs)


def again_moments(pairs):
    global_sum, global_square = local_moments(pairs, 0)
    local_sum, local_square = local_moments(pairs, 1)
    sums = lax.psum((global_sum, global_square, local_sum, local_square), ("dp", "grp"))
    return moment_list(sums, pairs)


def standard(value, moment):
    return (value - moment[0]) * moment[1]


def norm_back(items):
    parts = []
    for group in range(2):
        parts.append(jnp.concatenate([jnp.sum(item[0][group], axis=(0, 1, 2)) for item in items]))
        parts.append(
            jnp.concatenate(
                [jnp.sum(item[0][group] * item[1][group], axis=(0, 1, 2)) for item in items]
            )
        )
    sums = lax.psum((parts[0], parts[1], parts[2], parts[3]), ("dp", "grp"))
    devices = lax.axis_size(("dp", "grp"))
    results = []
    start = 0
    for grads, scaled, moments, gain in items:
        width = grads[0].shape[3]
        shift_grad = sums[0][start : start + width] + sums[2][start : start + width]
        gain_grad = sums[1][start : start + width] + sums[3][start : start + width]
        backs = []
        for group in range(2):
            count = grads[group].shape[0] * grads[group].shape[1] * grads[group].shape[2] * devices
            mean_grad = sums[2 * group][start : start + width] / count
            mean_cross = sums[2 * group + 1][start : start + width] / count
            value = (
                gain * moments[group][1] * (grads[group] - mean_grad - scaled[group] * mean_cross)
            )
            backs.append(value.astype(jnp.bfloat16))
        results.append((backs, gain_grad, shift_grad))
        start = start + width
    return results


def norm_section(hidden, moments, gain, shift):
    scaled = [standard(value, moment) for value, moment in zip(hidden, moments)]
    before = [value * gain + shift for value in scaled]
    return (scaled, before)


def project_forward(images, weights, norms, provide):
    w_reduce, w_spatial, w_expand, w_short = weights
    gain_mid, shift_mid, gain_wide, shift_wide = norms
    calls = []
    first = [mix(value, w_reduce) for value in images]
    moments1 = provide([first])
    calls.append(moments1)
    scaled1, before1 = norm_section(first, moments1[0], gain_mid[0], shift_mid[0])
    inner1 = [gelu(value).astype(jnp.bfloat16) for value in before1]
    rows1 = [patches(value, 2) for value in inner1]
    second = [mix(value, w_spatial) for value in rows1]
    moments2 = provide([second])
    calls.append(moments2)
    scaled2, before2 = norm_section(second, moments2[0], gain_mid[1], shift_mid[1])
    inner2 = [gelu(value).astype(jnp.bfloat16) for value in before2]
    third = [mix(value, w_expand) for value in inner2]
    strided = [value[:, ::2, ::2, :] for value in images]
    side = [mix(value, w_short) for value in strided]
    moments3 = provide([third, side])
    calls.append(moments3)
    scaled3, main_part = norm_section(third, moments3[0], gain_wide[0], shift_wide[0])
    scaled_side, side_part = norm_section(side, moments3[1], gain_wide[1], shift_wide[1])
    before_out = [main + branch for main, branch in zip(main_part, side_part)]
    result = [gelu(value).astype(jnp.bfloat16) for value in before_out]
    record = {
        "calls": calls,
        "images": images,
        "scaled1": scaled1,
        "before1": before1,
        "moments1": moments1[0],
        "inner1": inner1,
        "rows1": rows1,
        "scaled2": scaled2,
        "before2": before2,
        "moments2": moments2[0],
        "inner2": inner2,
        "strided": strided,
        "scaled3": scaled3,
        "moments3": moments3[0],
        "scaled_side": scaled_side,
        "moments_side": moments3[1],
        "before_out": before_out,
    }
    return (result, record)


def identity_forward(middle, weights, norms, provide):
    w_reduce2, w_spatial2, w_expand2 = weights
    gain_mid, shift_mid, gain_wide, shift_wide = norms
    calls = []
    fourth = [mix(value, w_reduce2) for value in middle]
    moments4 = provide([fourth])
    calls.append(moments4)
    scaled4, before4 = norm_section(fourth, moments4[0], gain_mid[2], shift_mid[2])
    inner4 = [gelu(value).astype(jnp.bfloat16) for value in before4]
    rows4 = [patches(value, 1) for value in inner4]
    fifth = [mix(value, w_spatial2) for value in rows4]
    moments5 = provide([fifth])
    calls.append(moments5)
    scaled5, before5 = norm_section(fifth, moments5[0], gain_mid[3], shift_mid[3])
    inner5 = [gelu(value).astype(jnp.bfloat16) for value in before5]
    sixth = [mix(value, w_expand2) for value in inner5]
    moments6 = provide([sixth])
    calls.append(moments6)
    scaled6, main_part = norm_section(sixth, moments6[0], gain_wide[2], shift_wide[2])
    before_out = [main + residual.astype(jnp.float32) for main, residual in zip(main_part, middle)]
    result = [gelu(value) for value in before_out]
    record = {
        "calls": calls,
        "middle": middle,
        "scaled4": scaled4,
        "before4": before4,
        "moments4": moments4[0],
        "inner4": inner4,
        "rows4": rows4,
        "scaled5": scaled5,
        "before5": before5,
        "moments5": moments5[0],
        "inner5": inner5,
        "scaled6": scaled6,
        "moments6": moments6[0],
        "before_out": before_out,
    }
    return (result, record)


def identity_back(incoming, record, weights, norms):
    w_reduce2, w_spatial2, w_expand2 = weights
    gain_mid, shift_mid, gain_wide, shift_wide = norms
    grad_before = [gelu_back(value, grad) for value, grad in zip(record["before_out"], incoming)]
    sixth_back = norm_back([(grad_before, record["scaled6"], record["moments6"], gain_wide[2])])[0]
    grad_expand2 = weight_term(record["inner5"], sixth_back[0])
    grad_inner5 = [mix_back(grad, w_expand2) for grad in sixth_back[0]]
    grad_before5 = [gelu_back(value, grad) for value, grad in zip(record["before5"], grad_inner5)]
    fifth_back = norm_back([(grad_before5, record["scaled5"], record["moments5"], gain_mid[3])])[0]
    grad_spatial2 = weight_term(record["rows4"], fifth_back[0])
    grad_inner4 = [
        unpatch(mix_back(grad, w_spatial2), value.shape, 1)
        for grad, value in zip(fifth_back[0], record["inner4"])
    ]
    grad_before4 = [gelu_back(value, grad) for value, grad in zip(record["before4"], grad_inner4)]
    fourth_back = norm_back([(grad_before4, record["scaled4"], record["moments4"], gain_mid[2])])[0]
    grad_reduce2 = weight_term(record["middle"], fourth_back[0])
    grad_middle = [
        mix_back(grad, w_reduce2) + residual for grad, residual in zip(fourth_back[0], grad_before)
    ]
    gains = (fourth_back[1], fifth_back[1], sixth_back[1])
    shifts = (fourth_back[2], fifth_back[2], sixth_back[2])
    return (grad_middle, (grad_reduce2, grad_spatial2, grad_expand2), gains, shifts)


def project_back(grad_middle, record, weights, norms):
    w_reduce, w_spatial, w_expand, w_short = weights
    gain_mid, shift_mid, gain_wide, shift_wide = norms
    grad_before = [gelu_back(value, grad) for value, grad in zip(record["before_out"], grad_middle)]
    main_back, side_back = norm_back(
        [
            (grad_before, record["scaled3"], record["moments3"], gain_wide[0]),
            (grad_before, record["scaled_side"], record["moments_side"], gain_wide[1]),
        ]
    )
    grad_expand = weight_term(record["inner2"], main_back[0])
    grad_short = weight_term(record["strided"], side_back[0])
    grad_inner2 = [mix_back(grad, w_expand) for grad in main_back[0]]
    grad_before2 = [gelu_back(value, grad) for value, grad in zip(record["before2"], grad_inner2)]
    second_back = norm_back([(grad_before2, record["scaled2"], record["moments2"], gain_mid[1])])[0]
    grad_spatial = weight_term(record["rows1"], second_back[0])
    grad_inner1 = [
        unpatch(mix_back(grad, w_spatial), value.shape, 2)
        for grad, value in zip(second_back[0], record["inner1"])
    ]
    grad_before1 = [gelu_back(value, grad) for value, grad in zip(record["before1"], grad_inner1)]
    first_back = norm_back([(grad_before1, record["scaled1"], record["moments1"], gain_mid[0])])[0]
    grad_reduce = weight_term(record["images"], first_back[0])
    grad_images = []
    for grad_first, grad_side in zip(first_back[0], side_back[0]):
        direct = mix_back(grad_first, w_reduce)
        across = mix_back(grad_side, w_short)
        direct = direct.at[:, ::2, ::2, :].add(across)
        grad_images.append(direct.astype(jnp.bfloat16))
    gains = (first_back[1], second_back[1], main_back[1], side_back[1])
    shifts = (first_back[2], second_back[2], main_back[2], side_back[2])
    return (grad_images, (grad_reduce, grad_spatial, grad_expand, grad_short), gains, shifts)


def body(
    image_global,
    image_local,
    w_reduce,
    w_spatial,
    w_expand,
    w_short,
    w_reduce2,
    w_spatial2,
    w_expand2,
    gain_mid,
    shift_mid,
    gain_wide,
    shift_wide,
    cotangent_global,
    cotangent_local,
):
    images = [image_global, image_local]
    first_weights = (w_reduce, w_spatial, w_expand, w_short)
    second_weights = (w_reduce2, w_spatial2, w_expand2)
    norms = (gain_mid, shift_mid, gain_wide, shift_wide)
    middle, first_record = project_forward(images, first_weights, norms, fresh_moments)
    final, second_record = identity_forward(middle, second_weights, norms, fresh_moments)
    incoming = [cotangent_global.astype(jnp.float32), cotangent_local.astype(jnp.float32)]
    unused, late_record = identity_forward(middle, second_weights, norms, again_moments)
    grad_middle, late_weights, late_gains, late_shifts = identity_back(
        incoming, late_record, second_weights, norms
    )
    unused, early_record = project_forward(images, first_weights, norms, again_moments)
    grad_images, early_weights, early_gains, early_shifts = project_back(
        grad_middle, early_record, first_weights, norms
    )
    shares = (
        lax.psum_scatter(early_weights[0], "dp", scatter_dimension=0, tiled=True),
        lax.psum_scatter(early_weights[1], "dp", scatter_dimension=0, tiled=True),
        lax.psum_scatter(early_weights[2], "dp", scatter_dimension=0, tiled=True),
        lax.psum_scatter(early_weights[3], "dp", scatter_dimension=0, tiled=True),
        lax.psum_scatter(late_weights[0], "dp", scatter_dimension=0, tiled=True),
        lax.psum_scatter(late_weights[1], "dp", scatter_dimension=0, tiled=True),
        lax.psum_scatter(late_weights[2], "dp", scatter_dimension=0, tiled=True),
    )
    totals = lax.psum(
        (shares[0], shares[1], shares[2], shares[3], shares[4], shares[5], shares[6]), "grp"
    )
    grad_gain_mid = jnp.stack([early_gains[0], early_gains[1], late_gains[0], late_gains[1]])
    grad_shift_mid = jnp.stack([early_shifts[0], early_shifts[1], late_shifts[0], late_shifts[1]])
    grad_gain_wide = jnp.stack([early_gains[2], early_gains[3], late_gains[2]])
    grad_shift_wide = jnp.stack([early_shifts[2], early_shifts[3], late_shifts[2]])
    return (
        final[0].astype(jnp.bfloat16),
        final[1].astype(jnp.bfloat16),
        grad_images[0],
        grad_images[1],
        totals[0],
        totals[1],
        totals[2],
        totals[3],
        totals[4],
        totals[5],
        totals[6],
        grad_gain_mid,
        grad_shift_mid,
        grad_gain_wide,
        grad_shift_wide,
    )


def solution(mesh):
    in_specs = (
        P(("dp", "grp"), None, None, None),
        P(("dp", "grp"), None, None, None),
        P(),
        P(),
        P(),
        P(),
        P(),
        P(),
        P(),
        P(),
        P(),
        P(),
        P(),
        P(("dp", "grp"), None, None, None),
        P(("dp", "grp"), None, None, None),
    )
    out_specs = (
        P(("dp", "grp"), None, None, None),
        P(("dp", "grp"), None, None, None),
        P(("dp", "grp"), None, None, None),
        P(("dp", "grp"), None, None, None),
        P("dp", None),
        P("dp", None),
        P("dp", None),
        P("dp", None),
        P("dp", None),
        P("dp", None),
        P("dp", None),
        P(),
        P(),
        P(),
        P(),
    )
    return jax.shard_map(body, mesh=mesh, in_specs=in_specs, out_specs=out_specs, check_vma=False)
```

profile of v0, /device:TPU:0, one launch (start us, length us, event | category | flops | bytes accessed | tf_op | source)
XLA Modules:
  0.0 1982.7 jit_solution(5492293906335933393)
XLA Ops:
  7.3 4.4 fusion.261
  14.6 42.0 %all-reduce.17 = (f32[512]{0:T(512)S(1)}, f32[512]{0:T(512)S(1)}, f32[512]{0:T(512)S(1)}, f32[512]{0:T(512)S(1)}) all-reduce(f32[512]{0:T(512)S(1)} %get-tuple-element.275, f32[512]{0:T(512)S(1)} %get-tuple-element.274, f32[512]{0:T(512)S(1)} %get-tuple-element.290, ...), channel_id=1, replica_groups=mesh['dp'=8,'grp'=4] {'dp','grp'}, use_global_device_ids=true, to_apply=%region_3.0 | all-reduce | flops 2048 | bytes 16384 | tf_op jit(solution)/shard_map/psum | solution.py:86
  61.5 13.7 slice.994
  75.2 13.7 slice.995
  89.0 13.7 slice.996
  102.7 13.7 slice.997
  116.5 13.7 slice.998
  130.2 10.9 slice.999
  141.1 10.9 slice.1000
  152.0 10.9 slice.1001
  163.0 10.9 slice.1002
  180.6 3.0 fusion.274
  186.5 3.4 fusion.260
  189.9 40.4 %all-reduce.16 = (f32[512]{0:T(512)S(1)}, f32[512]{0:T(512)S(1)}, f32[512]{0:T(512)S(1)}, f32[512]{0:T(512)S(1)}) all-reduce(f32[512]{0:T(512)S(1)} %get-tuple-element.302, f32[512]{0:T(512)S(1)} %get-tuple-element.301, f32[512]{0:T(512)S(1)} %copy-done.146, f32[512]{0:T(512)S(1)} %copy-done.145), channel_id=1, replica_groups=mesh['dp'=8,'grp'=4] {'dp','grp'}, use_global_device_ids=true, to_apply=%region_7.0 | all-reduce | flops 2048 | bytes 16384 | tf_op jit(solution)/shard_map/psum | solution.py:86
  245.1 111.8 %all-reduce.25.cloned.1.call-done = (f32[4096]{0:T(1024)}, f32[4096]{0:T(1024)}, f32[4096]{0:T(1024)}, f32[4096]{0:T(1024)}) async-done(((f32[4096]{0:T(1024)}, f32[4096]{0:T(1024)}, f32[4096]{0:T(1024)}, f32[4096]{0:T(1024)}), (f32[4096]{0:T(1024)}, f32[4096]{0:T(1024)}, f32[4096]{0:T(1024)}, f32[4096]{0:T(1024)})) %all-reduce.25.cloned.1.call-update) | async-done | bytes 65552 | tf_op jit(solution)/shard_map/psum | solution.py:86
  366.5 41.0 %all-reduce.14 = (f32[512]{0:T(512)S(1)}, f32[512]{0:T(512)S(1)}, f32[512]{0:T(512)S(1)}, f32[512]{0:T(512)S(1)}) all-reduce(f32[512]{0:T(512)S(1)} %get-tuple-element.300, f32[512]{0:T(512)S(1)} %get-tuple-element.299, f32[512]{0:T(512)S(1)} %get-tuple-element.312, ...), channel_id=1, replica_groups=mesh['dp'=8,'grp'=4] {'dp','grp'}, use_global_device_ids=true, to_apply=%region_17.18 | all-reduce | flops 2048 | bytes 16384 | tf_op jit(solution)/shard_map/psum | solution.py:86
  409.8 4.9 fusion.278
  414.8 3.0 fusion.272
  417.8 39.9 %all-reduce.13 = (f32[512]{0:T(512)S(1)}, f32[512]{0:T(512)S(1)}, f32[512]{0:T(512)S(1)}, f32[512]{0:T(512)S(1)}) all-reduce(f32[512]{0:T(512)S(1)} %get-tuple-element.298, f32[512]{0:T(512)S(1)} %get-tuple-element.297, f32[512]{0:T(512)S(1)} %get-tuple-element.310, ...), channel_id=1, replica_groups=mesh['dp'=8,'grp'=4] {'dp','grp'}, use_global_device_ids=true, to_apply=%region_21.22 | all-reduce | flops 2048 | bytes 16384 | tf_op jit(solution)/shard_map/psum | solution.py:86
  463.3 40.9 %all-reduce.12 = (f32[2048]{0:T(1024)S(1)}, f32[2048]{0:T(1024)S(1)}, f32[2048]{0:T(1024)S(1)}, f32[2048]{0:T(1024)S(1)}) all-reduce(f32[2048]{0:T(1024)S(1)} %get-tuple-element.269, f32[2048]{0:T(1024)S(1)} %get-tuple-element.268, f32[2048]{0:T(1024)S(1)} %get-tuple-element.284, ...), channel_id=1, replica_groups=mesh['dp'=8,'grp'=4] {'dp','grp'}, use_global_device_ids=true, to_apply=%region_25.26 | all-reduce | flops 8192 | bytes 65536 | tf_op jit(solution)/shard_map/psum | solution.py:86
  504.8 3.8 fusion.264
  508.7 3.7 fusion.257
  512.4 39.8 %all-reduce.11 = (f32[2048]{0:T(1024)S(1)}, f32[2048]{0:T(1024)S(1)}, f32[2048]{0:T(1024)S(1)}, f32[2048]{0:T(1024)S(1)}) all-reduce(f32[2048]{0:T(1024)S(1)} %get-tuple-element.267, f32[2048]{0:T(1024)S(1)} %get-tuple-element.266, f32[2048]{0:T(1024)S(1)} %get-tuple-element.282, ...), channel_id=1, replica_groups=mesh['dp'=8,'grp'=4] {'dp','grp'}, use_global_device_ids=true, to_apply=%region_55.56 | all-reduce | flops 8192 | bytes 65536 | tf_op jit(solution)/shard_map/psum | solution.py:110
  561.3 41.0 %all-reduce.10 = (f32[512]{0:T(512)S(1)}, f32[512]{0:T(512)S(1)}, f32[512]{0:T(512)S(1)}, f32[512]{0:T(512)S(1)}) all-reduce(f32[512]{0:T(512)} %get-tuple-element.296, f32[512]{0:T(512)} %get-tuple-element.295, f32[512]{0:T(512)} %get-tuple-element.308, f32[512]{0:T(512)S(1)} %copy-done.181), channel_id=1, replica_groups=mesh['dp'=8,'grp'=4] {'dp','grp'}, use_global_device_ids=true, to_apply=%region_59.60 | all-reduce | flops 2048 | bytes 16384 | tf_op jit(solution)/shard_map/psum | solution.py:110
  604.7 4.2 fusion.1
  618.7 3.9 scatter-add.231
  622.6 3.9 add_select_fusion
  626.5 4.0 scatter-add.232
  660.4 39.7 %all-reduce.9 = (f32[512]{0:T(512)S(1)}, f32[512]{0:T(512)S(1)}, f32[512]{0:T(512)S(1)}, f32[512]{0:T(512)S(1)}) all-reduce(f32[512]{0:T(512)S(1)} %get-tuple-element.294, f32[512]{0:T(512)S(1)} %get-tuple-element.293, f32[512]{0:T(512)S(1)} %get-tuple-element.306, ...), channel_id=1, replica_groups=mesh['dp'=8,'grp'=4] {'dp','grp'}, use_global_device_ids=true, to_apply=%region_64.65 | all-reduce | flops 2048 | bytes 16384 | tf_op jit(solution)/shard_map/psum | solution.py:110
  702.5 4.9 fusion.263
  708.4 4.1 fusion.256
  716.1 117.8 %all-reduce.23.cloned.1.call-done = (f32[4096]{0:T(1024)}, f32[4096]{0:T(1024)}, f32[4096]{0:T(1024)}, f32[4096]{0:T(1024)}) async-done(((f32[4096]{0:T(1024)}, f32[4096]{0:T(1024)}, f32[4096]{0:T(1024)}, f32[4096]{0:T(1024)}), (f32[4096]{0:T(1024)}, f32[4096]{0:T(1024)}, f32[4096]{0:T(1024)}, f32[4096]{0:T(1024)})) %all-reduce.23.cloned.1.call-update) | async-done | bytes 65552 | tf_op jit(solution)/shard_map/psum | solution.py:110
  836.6 3.1 multiply_convert_fusion.7
  846.0 41.2 %all-reduce.7 = (f32[512]{0:T(512)S(1)}, f32[512]{0:T(512)S(1)}, f32[512]{0:T(512)S(1)}, f32[512]{0:T(512)S(1)}) all-reduce(f32[512]{0:T(512)S(1)} %get-tuple-element.292, f32[512]{0:T(512)S(1)} %get-tuple-element.291, f32[512]{0:T(512)S(1)} %get-tuple-element.304, ...), channel_id=1, replica_groups=mesh['dp'=8,'grp'=4] {'dp','grp'}, use_global_device_ids=true, to_apply=%region_73.74 | all-reduce | flops 2048 | bytes 16384 | tf_op jit(solution)/shard_map/psum | solution.py:110
  888.5 4.1 fusion.9
  911.9 4.2 fusion.11
  926.3 6.2 scatter_fusion
  932.5 6.2 scatter_fusion.1
  938.7 6.2 scatter_fusion.2
  944.9 6.2 scatter_fusion.3
  951.1 6.2 scatter_fusion.4
  957.3 6.2 scatter_fusion.5
  963.5 6.2 scatter_fusion.6
  969.7 6.4 scatter_fusion.7
  976.1 6.2 scatter_fusion.8
  983.8 3.1 fusion.255
  986.8 39.5 %all-reduce.6 = (f32[512]{0:T(512)S(1)}, f32[512]{0:T(512)S(1)}, f32[512]{0:T(512)S(1)}, f32[512]{0:T(512)S(1)}) all-reduce(f32[512]{0:T(512)S(1)} %get-tuple-element.262, f32[512]{0:T(512)S(1)} %get-tuple-element.261, f32[512]{0:T(512)S(1)} %get-tuple-element.277, ...), channel_id=1, replica_groups=mesh['dp'=8,'grp'=4] {'dp','grp'}, use_global_device_ids=true, to_apply=%region_86.87 | all-reduce | flops 2048 | bytes 16384 | tf_op jit(solution)/shard_map/psum | solution.py:110
  1053.7 5.7 fusion
  1060.3 3.7 fusion.48
  1064.1 5.1 bitcast_add_fusion
  1070.1 3.7 fusion.50
  1073.8 5.1 bitcast_add_fusion.1
  1079.3 24.0 %reduce-scatter.8.cloned.1.call-done = f32[128,512]{0,1:T(8,128)} async-done(((f32[1024,512]{0,1:T(8,128)}), f32[128,512]{0,1:T(8,128)}) %reduce-scatter.8.cloned.1.call-update) | async-done | bytes 262160 | tf_op jit(solution)/shard_map/reduce_scatter | solution.py:316
  1103.3 90.4 %reduce-scatter.20.cloned.1.call-done = f32[64,2048]{1,0:T(8,128)} async-done(((f32[512,2048]{1,0:T(8,128)}), f32[64,2048]{1,0:T(8,128)}) %reduce-scatter.20.cloned.1.call-update) | async-done | bytes 524304 | tf_op jit(solution)/shard_map/reduce_scatter | solution.py:322
  1193.7 91.6 %reduce-scatter.16.cloned.1.call-done = f32[256,512]{1,0:T(8,128)} async-done(((f32[2048,512]{1,0:T(8,128)}), f32[256,512]{1,0:T(8,128)}) %reduce-scatter.16.cloned.1.call-update) | async-done | bytes 524304 | tf_op jit(solution)/shard_map/reduce_scatter | solution.py:320
  1285.4 91.3 %reduce-scatter.12.cloned.1.call-done = f32[64,2048]{1,0:T(8,128)} async-done(((f32[512,2048]{1,0:T(8,128)}), f32[64,2048]{1,0:T(8,128)}) %reduce-scatter.12.cloned.1.call-update) | async-done | bytes 524304 | tf_op jit(solution)/shard_map/reduce_scatter | solution.py:318
  1376.7 153.2 %reduce-scatter.14.cloned.1.call-done = f32[128,2048]{0,1:T(8,128)} async-done(((f32[1024,2048]{0,1:T(8,128)}), f32[128,2048]{0,1:T(8,128)}) %reduce-scatter.14.cloned.1.call-update) | async-done | bytes 1048592 | tf_op jit(solution)/shard_map/reduce_scatter | solution.py:319
  1529.9 166.0 %reduce-scatter.18.cloned.1.call-done = f32[576,512]{1,0:T(8,128)} async-done(((f32[4608,512]{1,0:T(8,128)}), f32[576,512]{1,0:T(8,128)}) %reduce-scatter.18.cloned.1.call-update) | async-done | bytes 1179664 | tf_op jit(solution)/shard_map/reduce_scatter | solution.py:321
  1696.0 166.0 %reduce-scatter.10.cloned.1.call-done = f32[576,512]{1,0:T(8,128)} async-done(((f32[4608,512]{1,0:T(8,128)}), f32[576,512]{1,0:T(8,128)}) %reduce-scatter.10.cloned.1.call-update) | async-done | bytes 1179664 | tf_op jit(solution)/shard_map/reduce_scatter | solution.py:317
  1868.5 3.2 scatter_fusion.19
  1875.9 3.8 copy.76
  1882.2 9.3 scatter_fusion.9
  1891.6 3.9 convert_element_type.140
  1898.1 69.4 %all-reduce.27.cloned.1.call-done = (f32[128,512]{0,1:T(8,128)}, f32[576,512]{1,0:T(8,128)}, f32[64,2048]{1,0:T(8,128)}, f32[128,2048]{0,1:T(8,128)}, f32[256,51...) async-done(((f32[128,512]{0,1:T(8,128)}, f32[576,512]{1,0:T(8,128)}, f32[64,2048]{1,0:T(8,128)}, f32[128,2048]{0,1:T(8,128)}, f32[256,512]{1,0:T(8,128)}, ...) | async-done | bytes 5242896 | tf_op jit(solution)/shard_map/psum | solution.py:324
  (643 shorter events, 200.6 us)
Async XLA Ops:
  7.2 355.5 %copy-start = (bf16[2048,512]{1,0:T(8,128)(2,1)S(1)}, bf16[2048,512]{1,0:T(8,128)(2,1)}, u32[]{:S(2)}) copy-start(bf16[2048,512]{1,0:T(8,128)(2,1)} %param.57) | copy-start | bytes 6291460
  7.2 349.7 %all-reduce.25.cloned.1.call-start = ((), (), s32[]{:S(2)}) async-start(), calls=%async_computation.15 | async-start | bytes 131072 | tf_op jit(solution)/shard_map/psum | solution.py:86
  14.0 219.3 %copy-start.105 = (f32[1,512]{1,0:T(1,128)}, f32[1,512]{1,0:T(1,128)S(1)}, u32[]{:S(2)}) copy-start(f32[1,512]{1,0:T(1,128)S(1)} %get-tuple-element.448) | copy-start | bytes 6148
  14.6 42.6 %copy-start.109 = (f32[1,512]{1,0:T(1,128)}, f32[1,512]{1,0:T(1,128)S(1)}, u32[]{:S(2)}) copy-start(f32[1,512]{1,0:T(1,128)S(1)} %get-tuple-element.453) | copy-start | bytes 6148
  60.2 118.0 %slice-start.4 = ((s8[4718592]{0:T(1024)(128)(4,1)}), s8[524288]{0:T(1024)(128)(4,1)S(1)}, s32[]{:S(2)}) async-start(s8[4718592]{0:T(1024)(128)(4,1)} %bitcast.365), calls=%async_computation.21 | async-start | bytes 1048576
  175.1 11.4 copy-start.93
  186.5 44.4 %copy-start.111 = (f32[1,512]{1,0:T(1,128)S(1)}, f32[1,512]{1,0:T(1,128)}, u32[]{:S(2)}) copy-start(f32[1,512]{1,0:T(1,128)} %get-tuple-element.452) | copy-start | bytes 6148
  233.3 126.4 %copy-start.6 = (f32[16,3,3,2048]{3,0,2,1:T(8,128)}, f32[16,3,3,2048]{3,0,2,1:T(8,128)S(1)}, u32[]{:S(2)}) copy-start(f32[16,3,3,2048]{3,0,2,1:T(8,128)S(1)} %get-tuple-element.540) | copy-start | bytes 3538948
  233.4 8.4 copy-start.134
  233.4 8.4 copy-start.135
  233.4 9.6 copy-start.192
  237.1 596.7 %all-reduce.23.cloned.1.call-start = ((), (), s32[]{:S(2)}) async-start(), calls=%async_computation.14 | async-start | bytes 131072 | tf_op jit(solution)/shard_map/psum | solution.py:110
  363.2 45.2 %copy-start.8 = (f32[16,3,3,512]{3,0,2,1:T(8,128)}, f32[16,3,3,512]{3,0,2,1:T(8,128)S(1)}, u32[]{:S(2)}) copy-start(f32[16,3,3,512]{3,0,2,1:T(8,128)S(1)} %get-tuple-element.542) | copy-start | bytes 884740
  366.5 42.6 %copy-start.20 = (f32[4,7,7,512]{3,2,1,0:T(8,128)}, f32[4,7,7,512]{3,2,1,0:T(8,128)S(1)}, u32[]{:S(2)}) copy-start(f32[4,7,7,512]{3,2,1,0:T(8,128)S(1)} %get-tuple-element.541) | copy-start | bytes 1204228
  408.2 6.6 slice-start
  414.7 43.0 %copy-start.107 = (f32[1,512]{1,0:T(1,128)S(1)}, f32[1,512]{1,0:T(1,128)}, u32[]{:S(2)}) copy-start(f32[1,512]{1,0:T(1,128)} %get-tuple-element.447) | copy-start | bytes 6148
  414.8 43.6 %copy-start.113 = (f32[1,512]{1,0:T(1,128)S(1)}, f32[1,512]{1,0:T(1,128)}, u32[]{:S(2)}) copy-start(f32[1,512]{1,0:T(1,128)} %get-tuple-element.451) | copy-start | bytes 6148
  558.5 45.1 %copy-start.40 = (f32[16,3,3,512]{3,0,2,1:T(8,128)S(1)}, f32[16,3,3,512]{3,0,2,1:T(8,128)}, u32[]{:S(2)}) copy-start(f32[16,3,3,512]{3,0,2,1:T(8,128)} %get-tuple-element.544) | copy-start | bytes 884740
  558.5 45.1 %copy-start.167 = (f32[512]{0:T(512)S(1)}, f32[512]{0:T(512)}, u32[]{:S(2)}) copy-start(f32[512]{0:T(512)} %get-tuple-element.467) | copy-start | bytes 6148
  558.5 50.6 %slice-start.2 = ((s8[4718592]{0:T(1024)(128)(4,1)}), s8[524288]{0:T(1024)(128)(4,1)S(1)}, s32[]{:S(2)}) async-start(s8[4718592]{0:T(1024)(128)(4,1)} %bitcast.363), calls=%async_computation.19 | async-start | bytes 1048576
  611.0 6.1 copy-start.4
  653.5 47.8 %copy-start.165 = (f32[512]{0:T(512)S(1)}, f32[512]{0:T(512)}, u32[]{:S(2)}) copy-start(f32[512]{0:T(512)} %get-tuple-element.463) | copy-start | bytes 6148
  702.5 5.7 copy-start.11
  702.5 5.7 copy-start.14
  708.2 6.2 copy-start.178
  708.2 6.2 copy-start.179
  708.2 6.2 copy-start.180
  708.2 6.2 copy-start.186
  708.2 6.2 copy-start.187
  708.3 6.2 copy-start.188
  708.3 6.2 copy-start.189
  708.3 6.2 copy-start.190
  708.3 6.2 copy-start.191
  708.3 7.1 copy-start.144
  708.3 7.1 copy-start.143
  708.3 7.2 copy-start.142
  708.3 7.3 copy-start.141
  708.3 7.4 copy-start.140
  708.3 7.4 copy-start.139
  708.4 7.5 copy-start.138
  708.4 7.6 copy-start.137
  708.4 7.7 copy-start.136
  708.4 128.2 %copy-start.7 = (f32[16,3,3,2048]{3,0,2,1:T(8,128)S(1)}, f32[16,3,3,2048]{3,0,2,1:T(8,128)}, u32[]{:S(2)}) copy-start(f32[16,3,3,2048]{3,0,2,1:T(8,128)} %copy-done.6) | copy-start | bytes 3538948
  708.4 128.2 %copy-start.119 = (f32[2048]{0:T(1024)S(1)}, f32[2048]{0:T(1024)}, u32[]{:S(2)}) copy-start(f32[2048]{0:T(1024)} %get-tuple-element.420) | copy-start | bytes 24580
  708.4 128.2 %copy-start.120 = (f32[2048]{0:T(1024)S(1)}, f32[2048]{0:T(1024)}, u32[]{:S(2)}) copy-start(f32[2048]{0:T(1024)} %get-tuple-element.421) | copy-start | bytes 24580
  714.4 388.9 %reduce-scatter.8.cloned.1.call-start = ((), (), s32[]{:S(2)}) async-start(), calls=%async_computation.7 | async-start | bytes 2359296 | tf_op jit(solution)/shard_map/reduce_scatter | solution.py:316
  843.8 44.5 %copy-start.37 = (f32[16,3,3,512]{3,0,2,1:T(8,128)S(1)}, f32[16,3,3,512]{3,0,2,1:T(8,128)}, u32[]{:S(2)}) copy-start(f32[16,3,3,512]{3,0,2,1:T(8,128)} %get-tuple-element.537) | copy-start | bytes 884740
  843.8 44.5 %copy-start.155 = (f32[512]{0:T(512)S(1)}, f32[512]{0:T(512)}, u32[]{:S(2)}) copy-start(f32[512]{0:T(512)} %get-tuple-element.459) | copy-start | bytes 6148
  902.5 6.4 copy-start.5
  902.5 6.4 copy-start.110
  902.6 6.4 copy-start.115
  902.6 6.4 copy-start.116
  983.8 43.7 %copy-start.3 = (f32[4,14,14,512]{3,2,1,0:T(8,128)S(1)}, f32[4,14,14,512]{3,2,1,0:T(8,128)}, u32[]{:S(2)}) copy-start(f32[4,14,14,512]{3,2,1,0:T(8,128)} %get-tuple-element.534) | copy-start | bytes 4816900
  983.8 43.7 %copy-start.148 = (f32[512]{0:T(512)S(1)}, f32[512]{0:T(512)}, u32[]{:S(2)}) copy-start(f32[512]{0:T(512)} %get-tuple-element.497) | copy-start | bytes 6148
  1034.8 158.9 %reduce-scatter.20.cloned.1.call-start = ((), (), s32[]{:S(2)}) async-start(), calls=%async_computation.13 | async-start | bytes 4718592 | tf_op jit(solution)/shard_map/reduce_scatter | solution.py:322
  1040.2 245.2 %reduce-scatter.16.cloned.1.call-start = ((), (), s32[]{:S(2)}) async-start(), calls=%async_computation.11 | async-start | bytes 4718592 | tf_op jit(solution)/shard_map/reduce_scatter | solution.py:320
  1045.2 331.5 %reduce-scatter.12.cloned.1.call-start = ((), (), s32[]{:S(2)}) async-start(), calls=%async_computation.9 | async-start | bytes 4718592 | tf_op jit(solution)/shard_map/reduce_scatter | solution.py:318
  1050.5 479.4 %reduce-scatter.14.cloned.1.call-start = ((), (), s32[]{:S(2)}) async-start(), calls=%async_computation.10 | async-start | bytes 9437184 | tf_op jit(solution)/shard_map/reduce_scatter | solution.py:319
  1059.4 636.5 %reduce-scatter.18.cloned.1.call-start = ((), (), s32[]{:S(2)}) async-start(), calls=%async_computation.12 | async-start | bytes 10616832 | tf_op jit(solution)/shard_map/reduce_scatter | solution.py:321
  1069.2 792.8 %reduce-scatter.10.cloned.1.call-start = ((), (), s32[]{:S(2)}) async-start(), calls=%async_computation.8 | async-start | bytes 10616832 | tf_op jit(solution)/shard_map/reduce_scatter | solution.py:317
  1079.0 888.5 %all-reduce.27.cloned.1.call-start = ((), (), s32[]{:S(2)}) async-start(), calls=%async_computation.16 | async-start | bytes 10485760 | tf_op jit(solution)/shard_map/psum | solution.py:324
  1891.6 5.9 copy-start.123
  1891.6 5.9 copy-start.126
  1891.6 5.8 copy-start.127
  (147 other events, 395.0 us)
Sparse Core Ops, SparseCore 0:
  237.3 119.5 all-reduce.24
  714.5 119.3 all-reduce.22
  1034.9 68.3 reduce-scatter.7
  1106.8 86.9 reduce-scatter.19
  1197.6 87.6 reduce-scatter.15
  1288.8 87.8 reduce-scatter.11
  1380.8 149.1 reduce-scatter.13
  1533.5 162.4 reduce-scatter.17
  1699.6 162.3 reduce-scatter.9
  1864.7 102.7 all-reduce.26
where the time goes:
time: 2010 us; the launch traced here: 1980 us
  waiting for transfers between devices  1080 us (54%)
  blocking collectives  406 us (20%)
  local copies, waits for them, and re-layouts  186 us (9%)
  other arithmetic  175 us (9%)
  matrix products  116 us (6%)
    psum x5, blocking collectives, fresh_moments(): lax.psum((global_sum, global_square, local_sum, local_square), ('dp', 'gr...  204 us
    psum x5, blocking collectives, norm_back(): sums = lax.psum((parts[0], parts[1], parts[2], parts[3]), ('dp', 'grp'))  201 us
    reduce_scatter x1, waiting for transfers between devices, body(): lax.psum_scatter(late_weights[1], 'dp', scatter_dimension=0, tiled=True)  166 us
    reduce_scatter x1, waiting for transfers between devices, body(): lax.psum_scatter(early_weights[1], 'dp', scatter_dimension=0, tiled=True)  166 us
    reduce_scatter x1, waiting for transfers between devices, body(): lax.psum_scatter(early_weights[3], 'dp', scatter_dimension=0, tiled=True)  153 us
    psum x1, waiting for transfers between devices, norm_back(): sums = lax.psum((parts[0], parts[1], parts[2], parts[3]), ('dp', 'grp'))  118 us
    slice x9, local copies, waits for them, and re-layouts, patches(): padded[:, row_tap:row_tap + reach:stride, col_tap:col_tap + reach:stride, :]  112 us
    psum x1, waiting for transfers between devices, fresh_moments(): lax.psum((global_sum, global_square, local_sum, local_square), ('dp', 'gr...  112 us
  transfers between devices with their start and end apart: 10, of which 10 were waited for; matrix products, arithmetic and copies ran while one was open for 4% of the time, Pallas kernels for 0%

commit v1 on v0

v1 whole, which is shorter than its diff:
```python
import functools

import jax
import jax.numpy as jnp
from jax import lax
from jax.experimental import pallas as pl
from jax.experimental.pallas import tpu as pltpu
from jax.sharding import PartitionSpec as P

EPS = 1e-05
MESH_ID = pl.DeviceIdType.MESH


def gelu(value):
    return jax.nn.gelu(value, approximate=True)


def gelu_back(before, grad):
    return jax.vjp(gelu, before)[1](grad)[0]


def stats_kernel(sizes, in_ref, out_ref, grp_buf, part, dp_buf, send_g, recv_g, send_d, recv_d):
    dp_size, grp_size = sizes
    dp = lax.axis_index("dp")
    grp = lax.axis_index("grp")
    barrier = pltpu.get_barrier_semaphore()
    for k in range(1, grp_size):
        pl.semaphore_signal(barrier, inc=1, device_id=(dp, grp ^ k), device_id_type=MESH_ID)
    for k in range(1, dp_size):
        pl.semaphore_signal(barrier, inc=1, device_id=(dp ^ k, grp), device_id_type=MESH_ID)
    pl.semaphore_wait(barrier, grp_size + dp_size - 2)
    copies = []
    for k in range(1, grp_size):
        copy = pltpu.make_async_remote_copy(
            src_ref=in_ref,
            dst_ref=grp_buf.at[grp],
            send_sem=send_g.at[k],
            recv_sem=recv_g.at[k],
            device_id=(dp, grp ^ k),
            device_id_type=MESH_ID,
        )
        copy.start()
        copies.append(copy)
    grp_buf[grp] = in_ref[...]
    for copy in copies:
        copy.wait()
    total = grp_buf[0]
    for k in range(1, grp_size):
        total = total + grp_buf[k]
    part[...] = total
    copies = []
    for k in range(1, dp_size):
        copy = pltpu.make_async_remote_copy(
            src_ref=part,
            dst_ref=dp_buf.at[dp],
            send_sem=send_d.at[k],
            recv_sem=recv_d.at[k],
            device_id=(dp ^ k, grp),
            device_id_type=MESH_ID,
        )
        copy.start()
        copies.append(copy)
    dp_buf[dp] = total
    for copy in copies:
        copy.wait()
    total = dp_buf[0]
    for k in range(1, dp_size):
        total = total + dp_buf[k]
    out_ref[...] = total


def all_sum(values):
    dp_size = lax.axis_size("dp")
    grp_size = lax.axis_size("grp")
    shape = values.shape
    number = {(4, 512): 1, (8, 2048): 2, (4, 2048): 3}[shape]
    return pl.pallas_call(
        functools.partial(stats_kernel, (dp_size, grp_size)),
        out_shape=jax.ShapeDtypeStruct(shape, jnp.float32),
        in_specs=[pl.BlockSpec(memory_space=pltpu.VMEM)],
        out_specs=pl.BlockSpec(memory_space=pltpu.VMEM),
        scratch_shapes=[
            pltpu.VMEM((grp_size,) + shape, jnp.float32),
            pltpu.VMEM(shape, jnp.float32),
            pltpu.VMEM((dp_size,) + shape, jnp.float32),
            pltpu.SemaphoreType.DMA((grp_size,)),
            pltpu.SemaphoreType.DMA((grp_size,)),
            pltpu.SemaphoreType.DMA((dp_size,)),
            pltpu.SemaphoreType.DMA((dp_size,)),
        ],
        compiler_params=pltpu.CompilerParams(collective_id=number, has_side_effects=True),
    )(values)


PANEL = 512
DEPTH = 8


def chunk_list(shapes, dp_size, half):
    chunks = []
    for number, (rows, columns) in enumerate(shapes):
        own = rows // dp_size
        for panel in range(columns // PANEL):
            for start in range(0, own, 2 * half):
                chunks.append((number, start, panel * PANEL))
    return chunks


class Reducer:
    def __init__(self, sizes, shapes, half, weights, outs, scratch):
        dp_size, grp_size = sizes
        self.half = half
        self.weights = weights
        self.outs = outs
        (
            self.acc,
            self.rc,
            self.rd,
            self.fin,
            self.load_sem,
            self.out_sem,
            self.send_sem,
            self.recv_sem,
            self.credit,
        ) = scratch
        self.chunks = chunk_list(shapes, dp_size, half)
        self.dp = lax.axis_index("dp")
        self.grp = lax.axis_index("grp")
        x_bits, dp_bits, y_bits = bit_counts(sizes)
        self.x_bits, self.dp_bits = x_bits, dp_bits
        self.orders = axis_orders(sizes)
        self.steps = x_bits + dp_bits
        self.groups = -(-len(self.chunks) // 3)
        self.stages = self.steps + x_bits + 3
        self.slots = self.steps + 2

    def bit(self, step):
        kind, index = step
        return ((self.grp >> (index + 1)) & 1) if kind == "x" else ((self.dp >> index) & 1)

    def partner(self, step):
        kind, index = step
        if kind == "x":
            return (self.dp, self.grp ^ (2 << index))
        return (self.dp ^ (1 << index), self.grp)

    def sibling(self):
        return (self.dp, self.grp ^ 1)

    def region(self, done, last_flip):
        place = [slice(None)] * self.dp_bits
        width = PANEL
        column = 0
        for number, step in enumerate(done):
            bit = self.bit(step)
            if last_flip and number == len(done) - 1:
                bit = 1 - bit
            if step[0] == "d":
                place[self.dp_bits - 1 - step[1]] = bit
            else:
                width = width // 2
                column = column + bit * width
        return place, column, width

    def view(self, ref, slot, done, flip=False):
        place, column, width = self.region(done, flip)
        if isinstance(column, int):
            cols = pl.ds(column, width)
        else:
            cols = pl.ds(pl.multiple_of(column, width), width)
        return ref.at[(slot, *place, slice(None), cols)]

    def landing(self, slot, order, count):
        return self.rd[slot % 3][count - 1].at[slot // 3]

    def c_copy(self, k, slot):
        number, start, column = self.chunks[k]
        source = self.weights[number].at[
            (slice(None),) * self.dp_bits
            + (
                pl.ds(start + (1 - self.grp % 2) * self.half, self.half),
                pl.ds(column, PANEL),
            )
        ]
        return pltpu.make_async_remote_copy(
            src_ref=source,
            dst_ref=self.rc.at[slot],
            send_sem=self.send_sem.at[slot, 0],
            recv_sem=self.recv_sem.at[slot, 0],
            device_id=self.sibling(),
            device_id_type=MESH_ID,
        )

    def load(self, k, slot):
        number, start, column = self.chunks[k]
        source = self.weights[number].at[
            (slice(None),) * self.dp_bits
            + (pl.ds(start + (self.grp % 2) * self.half, self.half), pl.ds(column, PANEL))
        ]
        return pltpu.make_async_copy(source, self.acc.at[slot], self.load_sem.at[slot])

    def d_copy(self, k, slot, count):
        order = self.orders[k % 3]
        return pltpu.make_async_remote_copy(
            src_ref=self.view(self.acc, slot, order[:count], True),
            dst_ref=self.landing(slot, order, count),
            send_sem=self.send_sem.at[slot, count],
            recv_sem=self.recv_sem.at[slot, count],
            device_id=self.partner(order[count - 1]),
            device_id_type=MESH_ID,
        )

    def x_columns(self, count):
        steps = [("x", i) for i in range(self.x_bits - count)]
        place, column, width = self.region(steps, False)
        if isinstance(column, int):
            return pl.ds(column, width)
        return pl.ds(pl.multiple_of(column, width), width)

    def ag_copy(self, k, slot, count):
        columns = self.x_columns(count)
        block = self.fin.at[slot, :, columns]
        stage = self.steps + 1 + count
        return pltpu.make_async_remote_copy(
            src_ref=block,
            dst_ref=block,
            send_sem=self.send_sem.at[slot, stage],
            recv_sem=self.recv_sem.at[slot, stage],
            device_id=self.partner(("x", self.x_bits - 1 - count)),
            device_id_type=MESH_ID,
        )

    def out_block(self, k):
        number, start, column = self.chunks[k]
        return self.outs[number].at[
            pl.ds(start + (self.grp % 2) * self.half, self.half), pl.ds(column, PANEL)
        ]

    def out_copies(self, k, slot):
        stage = self.stages - 2
        remote = pltpu.make_async_remote_copy(
            src_ref=self.fin.at[slot],
            dst_ref=self.out_block(k),
            send_sem=self.send_sem.at[slot, stage],
            recv_sem=self.recv_sem.at[slot, stage],
            device_id=self.sibling(),
            device_id_type=MESH_ID,
        )
        local = pltpu.make_async_copy(self.fin.at[slot], self.out_block(k), self.out_sem.at[slot])
        return remote, local

    def later(self, k):
        return k + 3 * self.slots < len(self.chunks)

    def give(self, k, slot, stage, device):
        if self.later(k):
            pl.semaphore_signal(
                self.credit.at[slot, stage], inc=1, device_id=device, device_id_type=MESH_ID
            )

    def take(self, k, slot, stage):
        if k >= 3 * self.slots:
            pl.semaphore_wait(self.credit.at[slot, stage], 1)

    def add(self, slot, order, count, target=None):
        done = order[:count]
        place, column, width = self.region(done, False)
        free = [number for number, value in enumerate(place) if isinstance(value, slice)]
        cols = pl.ds(column, width)
        if not isinstance(column, int):
            cols = pl.ds(pl.multiple_of(column, width), width)

        def one(index, carry):
            where = list(place)
            lead = []
            for position, axis in enumerate(free):
                value = (index >> (len(free) - 1 - position)) & 1
                where[axis] = value
                lead.append(value)
            if count == 0:
                arrived = self.rc[(slot, *lead)]
            else:
                arrived = self.rd[slot % 3][count - 1][(slot // 3, *lead)]
            here = (slot, *where, slice(None), cols)
            if target is None:
                self.acc[here] = self.acc[here] + arrived
            else:
                self.fin[slot, :, self.x_columns(0)] = self.acc[here] + arrived
            return carry

        total = 2 ** len(free)
        if total == 1:
            one(0, 0)
        else:
            lax.fori_loop(0, total, one, 0)

    def run(self, k, stage):
        slot = k % (3 * self.slots)
        order = self.orders[k % 3]
        steps = self.steps
        if stage == 0:
            self.load(k, slot).start()
            self.take(k, slot, 0)
            self.c_copy(k, slot).start()
        elif stage <= steps + 1:
            count = stage - 1
            if count == 0:
                self.load(k, slot).wait()
                self.c_copy(k, slot).wait()
            else:
                self.d_copy(k, slot, count).wait()
            self.add(slot, order, count, None if count < steps else True)
            device = self.sibling() if count == 0 else self.partner(order[count - 1])
            self.give(k, slot, count, device)
            self.take(k, slot, count + 1)
            if count < steps:
                self.d_copy(k, slot, count + 1).start()
            else:
                self.ag_copy(k, slot, 0).start()
        elif stage <= steps + self.x_bits:
            count = stage - steps - 1
            self.ag_copy(k, slot, count - 1).wait()
            self.take(k, slot, stage)
            self.ag_copy(k, slot, count).start()
        elif stage == self.stages - 2:
            self.ag_copy(k, slot, self.x_bits - 1).wait()
            remote, local = self.out_copies(k, slot)
            remote.start()
            local.start()
        else:
            remote, local = self.out_copies(k, slot)
            remote.wait()
            local.wait()
            for count in range(self.x_bits):
                device = self.partner(("x", self.x_bits - 1 - count))
                self.give(k, slot, steps + 1 + count, device)

    def step(self, time):
        for stage in reversed(range(self.stages)):
            group = time - stage
            if 0 <= group < self.groups:
                for k in range(3 * group, min(3 * group + 3, len(self.chunks))):
                    self.run(k, stage)

    def barrier(self):
        semaphore = pltpu.get_barrier_semaphore()
        devices = [self.sibling()] + [self.partner(step) for step in self.orders[0]]
        for device in devices:
            pl.semaphore_signal(semaphore, inc=1, device_id=device, device_id_type=MESH_ID)
        pl.semaphore_wait(semaphore, len(devices))


def bit_counts(sizes):
    dp_size, grp_size = sizes
    x_bits = (grp_size // 2).bit_length() - 1
    dp_bits = dp_size.bit_length() - 1
    return x_bits, dp_bits, x_bits


def axis_orders(sizes):
    x_bits, dp_bits, y_bits = bit_counts(sizes)
    xs = [("x", i) for i in range(x_bits)]
    ys = [("d", i) for i in range(y_bits)]
    zs = [("d", i) for i in range(y_bits, dp_bits)]
    return [xs + ys + zs, ys + zs[:1] + xs + zs[1:], zs[:1] + ys + xs + zs[1:]]


def reducer_scratch(sizes, half):
    x_bits, dp_bits, _ = bit_counts(sizes)
    steps = x_bits + dp_bits
    groups = steps + 2
    slots = 3 * groups
    stages = steps + x_bits + 3
    landings = []
    for order in axis_orders(sizes):
        for count in range(1, steps + 1):
            done = [step[0] for step in order[:count]]
            lead = (2,) * (dp_bits - done.count("d"))
            width = PANEL >> done.count("x")
            landings.append(pltpu.VMEM((groups,) + lead + (half, width), jnp.float32))
    block = (slots,) + (2,) * dp_bits + (half, PANEL)
    return [
        pltpu.VMEM(block, jnp.float32),
        pltpu.VMEM(block, jnp.float32),
        *landings,
        pltpu.VMEM((slots, half, PANEL), jnp.float32),
        pltpu.SemaphoreType.DMA((slots,)),
        pltpu.SemaphoreType.DMA((slots,)),
        pltpu.SemaphoreType.DMA((slots, stages)),
        pltpu.SemaphoreType.DMA((slots, stages)),
        pltpu.SemaphoreType.REGULAR((slots, stages)),
    ]


def reduce_kernel(sizes, shapes, half, *refs):
    count = len(shapes)
    x_bits, dp_bits, _ = bit_counts(sizes)
    weights = refs[:count]
    outs = refs[count : 2 * count]
    rest = refs[2 * count :]
    steps = x_bits + dp_bits
    landings = [rest[2 + steps * i : 2 + steps * (i + 1)] for i in range(3)]
    scratch = (rest[0], rest[1], landings) + tuple(rest[2 + 3 * steps :])
    reducer = Reducer(sizes, shapes, half, weights, outs, scratch)
    reducer.barrier()
    for time in range(reducer.groups + reducer.stages - 1):
        reducer.step(time)


def reduce_weights(grads):
    sizes = (lax.axis_size("dp"), lax.axis_size("grp"))
    dp_size = sizes[0]
    dp_bits = dp_size.bit_length() - 1
    shapes = [grad.shape for grad in grads]
    half = 256 // dp_size
    views = [
        grad.reshape((2,) * dp_bits + (grad.shape[0] // dp_size, grad.shape[1])) for grad in grads
    ]
    anywhere = pl.BlockSpec(memory_space=pl.ANY)
    return pl.pallas_call(
        functools.partial(reduce_kernel, sizes, shapes, half),
        out_shape=[
            jax.ShapeDtypeStruct((shape[0] // dp_size, shape[1]), jnp.float32) for shape in shapes
        ],
        in_specs=[anywhere] * len(grads),
        out_specs=[anywhere] * len(grads),
        scratch_shapes=reducer_scratch(sizes, half),
        compiler_params=pltpu.CompilerParams(
            collective_id=4, has_side_effects=True, vmem_limit_bytes=58 * 2**20
        ),
    )(*views)


def mix(value, weight):
    return jnp.einsum("nhwc,cd->nhwd", value, weight, preferred_element_type=jnp.float32)


def mix_back(grad, weight):
    return jnp.einsum("nhwd,cd->nhwc", grad, weight, preferred_element_type=jnp.float32)


def weight_term(values, grads):
    total = None
    for value, grad in zip(values, grads):
        term = jnp.einsum("nhwc,nhwd->cd", value, grad, preferred_element_type=jnp.float32)
        total = term if total is None else total + term
    return total


def spatial(value, weight, stride):
    kernel = weight.reshape(3, 3, value.shape[3], weight.shape[1])
    return lax.conv_general_dilated(
        value,
        kernel,
        (stride, stride),
        ((1, 1), (1, 1)),
        dimension_numbers=("NHWC", "HWIO", "NHWC"),
        preferred_element_type=jnp.float32,
    )


def spatial_back(grad, weight, stride):
    kernel = weight.reshape(3, 3, -1, weight.shape[1])[::-1, ::-1]
    return lax.conv_general_dilated(
        grad,
        kernel,
        (1, 1),
        ((1, stride), (1, stride)),
        lhs_dilation=(stride, stride),
        dimension_numbers=("NHWC", "HWOI", "NHWC"),
        preferred_element_type=jnp.float32,
    )


def spatial_weight(values, grads, stride):
    total = None
    for value, grad in zip(values, grads):
        high = 2 - stride
        term = lax.conv_general_dilated(
            value,
            grad,
            (1, 1),
            ((1, high), (1, high)),
            rhs_dilation=(stride, stride),
            dimension_numbers=("CHWN", "IHWO", "HWNC"),
            preferred_element_type=jnp.float32,
        )
        total = term if total is None else total + term
    return total.reshape(-1, total.shape[3])


def fresh_moments(pairs):
    rows = []
    for group in range(2):
        rows.append(jnp.concatenate([jnp.sum(pair[group], axis=(0, 1, 2)) for pair in pairs]))
        rows.append(
            jnp.concatenate([jnp.sum(pair[group] * pair[group], axis=(0, 1, 2)) for pair in pairs])
        )
    sums = spread_sum(rows, len(pairs))
    devices = lax.axis_size(("dp", "grp"))
    result = []
    start = 0
    for pair in pairs:
        width = pair[0].shape[3]
        moments = []
        for group in range(2):
            count = pair[group].shape[0] * pair[group].shape[1] * pair[group].shape[2] * devices
            mean = sums[2 * group][start : start + width] / count
            spread = sums[2 * group + 1][start : start + width] / count - mean * mean
            moments.append((mean, lax.rsqrt(spread + EPS)))
        result.append(moments)
        start = start + width
    return result


def spread_sum(rows, parts):
    stacked = jnp.stack(rows)
    width = stacked.shape[1] // parts
    stacked = stacked.reshape(4 * parts, width)
    return all_sum(stacked).reshape(4, parts * width)


def standard(value, moment):
    return (value - moment[0]) * moment[1]


def norm_back(items):
    rows = []
    for group in range(2):
        rows.append(jnp.concatenate([jnp.sum(item[0][group], axis=(0, 1, 2)) for item in items]))
        rows.append(
            jnp.concatenate(
                [jnp.sum(item[0][group] * item[1][group], axis=(0, 1, 2)) for item in items]
            )
        )
    sums = spread_sum(rows, len(items))
    devices = lax.axis_size(("dp", "grp"))
    results = []
    start = 0
    for grads, scaled, moments, gain in items:
        width = grads[0].shape[3]
        shift_grad = sums[0][start : start + width] + sums[2][start : start + width]
        gain_grad = sums[1][start : start + width] + sums[3][start : start + width]
        backs = []
        for group in range(2):
            count = grads[group].shape[0] * grads[group].shape[1] * grads[group].shape[2] * devices
            mean_grad = sums[2 * group][start : start + width] / count
            mean_cross = sums[2 * group + 1][start : start + width] / count
            value = (
                gain * moments[group][1] * (grads[group] - mean_grad - scaled[group] * mean_cross)
            )
            backs.append(value.astype(jnp.bfloat16))
        results.append((backs, gain_grad, shift_grad))
        start = start + width
    return results


def norm_section(hidden, moments, gain, shift):
    scaled = [standard(value, moment) for value, moment in zip(hidden, moments)]
    before = [value * gain + shift for value in scaled]
    return (scaled, before)


def rounded(values):
    return [value.astype(jnp.bfloat16) for value in values]


def body(
    image_global,
    image_local,
    w_reduce,
    w_spatial,
    w_expand,
    w_short,
    w_reduce2,
    w_spatial2,
    w_expand2,
    gain_mid,
    shift_mid,
    gain_wide,
    shift_wide,
    cotangent_global,
    cotangent_local,
):
    images = [image_global, image_local]
    first = [mix(value, w_reduce) for value in images]
    moments1 = fresh_moments([first])[0]
    scaled1, before1 = norm_section(first, moments1, gain_mid[0], shift_mid[0])
    inner1 = rounded([gelu(value) for value in before1])
    second = [spatial(value, w_spatial, 2) for value in inner1]
    moments2 = fresh_moments([second])[0]
    scaled2, before2 = norm_section(second, moments2, gain_mid[1], shift_mid[1])
    inner2 = rounded([gelu(value) for value in before2])
    third = [mix(value, w_expand) for value in inner2]
    strided = [value[:, ::2, ::2, :] for value in images]
    side = [mix(value, w_short) for value in strided]
    moments3, moments_side = fresh_moments([third, side])
    scaled3, main_part = norm_section(third, moments3, gain_wide[0], shift_wide[0])
    scaled_side, side_part = norm_section(side, moments_side, gain_wide[1], shift_wide[1])
    before_mid = [main + branch for main, branch in zip(main_part, side_part)]
    middle = rounded([gelu(value) for value in before_mid])
    fourth = [mix(value, w_reduce2) for value in middle]
    moments4 = fresh_moments([fourth])[0]
    scaled4, before4 = norm_section(fourth, moments4, gain_mid[2], shift_mid[2])
    inner4 = rounded([gelu(value) for value in before4])
    fifth = [spatial(value, w_spatial2, 1) for value in inner4]
    moments5 = fresh_moments([fifth])[0]
    scaled5, before5 = norm_section(fifth, moments5, gain_mid[3], shift_mid[3])
    inner5 = rounded([gelu(value) for value in before5])
    sixth = [mix(value, w_expand2) for value in inner5]
    moments6 = fresh_moments([sixth])[0]
    scaled6, main_part = norm_section(sixth, moments6, gain_wide[2], shift_wide[2])
    before_out = [main + residual.astype(jnp.float32) for main, residual in zip(main_part, middle)]
    final = rounded([gelu(value) for value in before_out])

    incoming = [cotangent_global.astype(jnp.float32), cotangent_local.astype(jnp.float32)]
    grad_out = [gelu_back(value, grad) for value, grad in zip(before_out, incoming)]
    back6, gain6, shift6 = norm_back([(grad_out, scaled6, moments6, gain_wide[2])])[0]
    grad_expand2 = weight_term(inner5, back6)
    grad5 = [gelu_back(u, mix_back(grad, w_expand2)) for u, grad in zip(before5, back6)]
    back5, gain5, shift5 = norm_back([(grad5, scaled5, moments5, gain_mid[3])])[0]
    grad_spatial2 = spatial_weight(inner4, back5, 1)
    grad4 = [gelu_back(u, spatial_back(grad, w_spatial2, 1)) for u, grad in zip(before4, back5)]
    back4, gain4, shift4 = norm_back([(grad4, scaled4, moments4, gain_mid[2])])[0]
    grad_reduce2 = weight_term(middle, back4)
    grad_middle = [mix_back(grad, w_reduce2) + rest for grad, rest in zip(back4, grad_out)]
    grad_join = [gelu_back(u, grad) for u, grad in zip(before_mid, grad_middle)]
    (back3, gain3, shift3), (back_side, gain_side, shift_side) = norm_back(
        [
            (grad_join, scaled3, moments3, gain_wide[0]),
            (grad_join, scaled_side, moments_side, gain_wide[1]),
        ]
    )
    grad_expand = weight_term(inner2, back3)
    grad_short = weight_term(strided, back_side)
    grad2 = [gelu_back(u, mix_back(grad, w_expand)) for u, grad in zip(before2, back3)]
    back2, gain2, shift2 = norm_back([(grad2, scaled2, moments2, gain_mid[1])])[0]
    grad_spatial = spatial_weight(inner1, back2, 2)
    grad1 = [gelu_back(u, spatial_back(grad, w_spatial, 2)) for u, grad in zip(before1, back2)]
    back1, gain1, shift1 = norm_back([(grad1, scaled1, moments1, gain_mid[0])])[0]
    grad_reduce = weight_term(images, back1)
    grad_images = []
    for grad_first, grad_side in zip(back1, back_side):
        direct = mix_back(grad_first, w_reduce)
        across = mix_back(grad_side, w_short)
        spread = lax.pad(across, jnp.float32(0), ((0, 0, 0), (0, 1, 1), (0, 1, 1), (0, 0, 0)))
        grad_images.append((direct + spread).astype(jnp.bfloat16))
    totals = reduce_weights(
        [
            grad_expand2,
            grad_spatial2,
            grad_reduce2,
            grad_expand,
            grad_short,
            grad_spatial,
            grad_reduce,
        ]
    )
    return (
        final[0],
        final[1],
        grad_images[0],
        grad_images[1],
        totals[6],
        totals[5],
        totals[3],
        totals[4],
        totals[2],
        totals[1],
        totals[0],
        jnp.stack([gain1, gain2, gain4, gain5]),
        jnp.stack([shift1, shift2, shift4, shift5]),
        jnp.stack([gain3, gain_side, gain6]),
        jnp.stack([shift3, shift_side, shift6]),
    )


def solution(mesh):
    crops = P(("dp", "grp"), None, None, None)
    in_specs = (crops, crops) + (P(),) * 11 + (crops, crops)
    out_specs = (crops,) * 4 + (P("dp", None),) * 7 + (P(),) * 4
    return jax.shard_map(body, mesh=mesh, in_specs=in_specs, out_specs=out_specs, check_vma=False)
```

time: 2010 us -> 583 us (0.29)
  waiting for transfers between devices: 1080 us -> 0 us
  blocking collectives: 406 us -> 0 us
  Pallas kernels: 0 us -> 345 us
  local copies, waits for them, and re-layouts: 186 us -> 39.4 us
  other arithmetic: 175 us -> 64 us
    reduce_scatter x7 -> x0, waiting for transfers between devices: 783 us -> none  [the longest x1 166 us: body(): lax.psum_scatter(late_weights[1], 'dp', scatter_dimension=0, tiled=True)]
    psum x10 -> x0, blocking collectives: 406 us -> none  [the longest x5 204 us: fresh_moments(): lax.psum((global_sum, global_square, local_sum, local_square), ('dp', 'gr...]
    pallas_call x0 -> x13, Pallas kernels: none -> 345 us  [the longest x1 184 us: reduce_weights(): pl.pallas_call(functools.partial(reduce_kernel, sizes, shapes, half), out...]
    psum x3 -> x0, waiting for transfers between devices: 299 us -> none  [the longest x1 118 us: norm_back(): sums = lax.psum((parts[0], parts[1], parts[2], parts[3]), ('dp', 'grp'))]
    slice x28 -> x5, local copies, waits for them, and re-layouts: 126 us -> 3.03 us  [the longest x1 1.15 us: body(): strided = [value[:, ::2, ::2, :] for value in images]]
    scatter-add x28 -> x0, other arithmetic: 87 us -> none  [the longest x26 74.4 us: unpatch(): total = total.at[:, row_tap:row_tap + reach:stride, col_tap:col_tap + rea...]
    conv_general_dilated x0 -> x12, matrix products: none -> 47.2 us  [the longest x4 16 us: spatial_back(): lax.conv_general_dilated(grad, kernel, (1, 1), ((1, stride), (1, stride))...]
    scatter-add x10 -> x0, local copies, waits for them, and re-layouts: 24.4 us -> none  [unpatch(): total = total.at[:, row_tap:row_tap + reach:stride, col_tap:col_tap + rea...]
  transfers between devices with their start and end apart: 10 -> 0, of which waited for: 10 -> 0; matrix products, arithmetic and copies ran while one was open for 4% -> 0% of each run, Pallas kernels for 0% -> 0%
where the time goes in v1:
time: 583 us; the launch traced here: 572 us
  Pallas kernels  345 us (59%)
  matrix products  121 us (21%)
  other arithmetic  64 us (11%)
  local copies, waits for them, and re-layouts  39.4 us (7%)
    pallas_call x1, Pallas kernels, reduce_weights(): pl.pallas_call(functools.partial(reduce_kernel, sizes, shapes, half), out...  184 us
    pallas_call x12, Pallas kernels, all_sum(): pl.pallas_call(functools.partial(stats_kernel, (dp_size, grp_size)), out_...  161 us
    dot_general x10, matrix products, mix(): jnp.einsum('nhwc,cd->nhwd', value, weight, preferred_element_type=jnp.flo...  25.6 us
    dot_general x10, matrix products, mix_back(): jnp.einsum('nhwd,cd->nhwc', grad, weight, preferred_element_type=jnp.floa...  24.8 us
    dot_general x10, matrix products, weight_term(): jnp.einsum('nhwc,nhwd->cd', value, grad, preferred_element_type=jnp.float32)  23 us
    unnamed x379, local copies, waits for them, and re-layouts  16.7 us
    convert_element_type x12, other arithmetic, norm_back(): backs.append(value.astype(jnp.bfloat16))  16.3 us
    conv_general_dilated x4, matrix products, spatial_back(): lax.conv_general_dilated(grad, kernel, (1, 1), ((1, stride), (1, stride))...  16 us

profile of v1, /device:TPU:0, one launch (start us, length us, event | category | flops | bytes accessed | tf_op | source)
XLA Modules:
  0.0 572.2 jit_solution(8454376373660171713)
XLA Ops:
  2.6 4.3 fusion.179
  6.9 1.8 fusion.180
  8.8 2.5 fusion.173
  11.9 13.4 %shard_map.262 = f32[4,512]{1,0:T(4,128)} custom-call(f32[4,512]{1,0:T(4,128)} %pad_maximum_fusion.14.in_ref), custom_call_target="tpu_custom_call" | custom-call | tf_op jit(solution)/shard_map/pallas_call | solution.py:77
  26.8 3.9 fusion.192
  31.6 3.1 fusion.186
  35.4 11.3 %shard_map.263 = f32[4,512]{1,0:T(4,128)} custom-call(f32[4,512]{1,0:T(4,128)} %pad_maximum_fusion.15.in_ref), custom_call_target="tpu_custom_call" | custom-call | tf_op jit(solution)/shard_map/pallas_call | solution.py:77
  48.2 3.4 fusion.178
  52.7 3.3 fusion.172
  56.5 2.3 fusion.171
  59.5 20.0 %shard_map.264 = f32[8,2048]{1,0:T(8,128)} custom-call(f32[8,2048]{1,0:T(8,128)} %reshape.756.in_ref), custom_call_target="tpu_custom_call" | custom-call | tf_op jit(solution)/shard_map/pallas_call | solution.py:77
  82.1 2.7 multiply_convert_fusion.12
  87.4 1.9 fusion.181
  89.8 12.2 %shard_map.265 = f32[4,512]{1,0:T(4,128)} custom-call(f32[4,512]{1,0:T(4,128)} %pad_maximum_fusion.16.in_ref), custom_call_target="tpu_custom_call" | custom-call | tf_op jit(solution)/shard_map/pallas_call | solution.py:77
  103.6 4.0 fusion.190
  107.6 4.5 fusion.185
  112.8 10.7 %shard_map.266 = f32[4,512]{1,0:T(4,128)} custom-call(f32[4,512]{1,0:T(4,128)} %pad_maximum_fusion.17.in_ref), custom_call_target="tpu_custom_call" | custom-call | tf_op jit(solution)/shard_map/pallas_call | solution.py:77
  125.0 3.4 fusion.177
  128.9 2.3 fusion.170
  131.8 14.8 %shard_map.267 = f32[4,2048]{1,0:T(4,128)} custom-call(f32[4,2048]{1,0:T(4,128)} %pad_maximum_fusion.2.in_ref), custom_call_target="tpu_custom_call" | custom-call | tf_op jit(solution)/shard_map/pallas_call | solution.py:77
  147.6 5.5 fusion.169
  154.7 2.9 fusion.176
  158.3 14.3 %shard_map.268 = f32[4,2048]{1,0:T(4,128)} custom-call(f32[4,2048]{1,0:T(4,128)} %pad_maximum_fusion.3.in_ref), custom_call_target="tpu_custom_call" | custom-call | tf_op jit(solution)/shard_map/pallas_call | solution.py:77
  174.2 2.6 multiply_convert_fusion.3
  178.1 1.6 fusion.184
  180.4 1.7 fusion.189
  182.7 11.2 %shard_map.269 = f32[4,512]{1,0:T(4,128)} custom-call(f32[4,512]{1,0:T(4,128)} %pad_maximum_fusion.18.in_ref), custom_call_target="tpu_custom_call" | custom-call | tf_op jit(solution)/shard_map/pallas_call | solution.py:77
  196.8 5.9 %fusion.183 = (f32[512]{0:T(512)S(1)}, f32[512]{0:T(512)S(1)}, f32[4,7,7,512]{3,0,2,1:T(4,128)}) fusion(f32[512]{0:T(512)} %copy-done.165, f32[512]{0:T(512)} %bitcast.476, f32[4,7,7,512]{3,2,1,0:T(8,128)} %get-tuple-element.247, f32[512]{0:T(512)S(1)} %bitcast.371, f32[512]{0:T(512)S(1)} %bitcast.330, ...), kind=kOutput, calls=%fused_computation.404 | convolution fusion | flops 759680000 | bytes 5734400 | tf_op jit(solution)/shard_map/conv_general_dilated | solution.py:464
  202.8 2.5 fusion.188
  205.9 10.7 %shard_map.270 = f32[4,512]{1,0:T(4,128)} custom-call(f32[4,512]{1,0:T(4,128)} %pad_maximum_fusion.19.in_ref), custom_call_target="tpu_custom_call" | custom-call | tf_op jit(solution)/shard_map/pallas_call | solution.py:77
  219.7 6.3 %fusion.168 = (f32[2048]{0:T(1024)S(1)}, f32[2048]{0:T(1024)S(1)}, f32[2048]{0:T(1024)S(1)}, f32[4,7,7,2048]{3,2,1,0:T(8,128)}) fusion(f32[2048]{0:T(1024)} %copy-done.107, f32[4,7,7,2048]{3,2,1,0:T(8,128)} %get-tuple-element.244, f32[2048]{0:T(1024)S(1)} %bitcast.344, f32[2048]{0:T(1024)} %copy-done.109, f32[4,7,7,2048]{3,2,1,0:T(8,128)} %get-tuple-element.245, ...), kind=kOutput, calls=%fused_computation.389 | convolution fusion | flops 424683520 | bytes 8810496 | tf_op jit(solution)/shard_map/nhwd,cd->nhwc/dot_general | solution.py:439
  226.3 2.9 fusion.175
  229.9 20.0 %shard_map.271 = f32[8,2048]{1,0:T(8,128)} custom-call(f32[8,2048]{1,0:T(8,128)} %reshape.758.in_ref), custom_call_target="tpu_custom_call" | custom-call | tf_op jit(solution)/shard_map/pallas_call | solution.py:77
  249.9 1.9 slice_add_fusion.3
  251.9 4.5 multiply_convert_fusion.2
  256.4 1.8 fusion.2
  258.3 10.6 %pad.6 = f32[4,14,14,1024]{3,2,1,0:T(8,128)} pad(f32[4,7,7,1024]{3,2,1,0:T(8,128)S(1)} %fusion.2, f32[]{:T(128)} %constant.107.clone.1), padding=0_0_0x0_1_1x0_1_1x0_0_0 | pad | bytes 4014084 | tf_op jit(solution)/shard_map/pad | solution.py:646
  269.0 3.1 fusion.25
  272.1 1.6 fusion.182
  275.6 1.7 fusion.187
  277.9 11.5 %shard_map.272 = f32[4,512]{1,0:T(4,128)} custom-call(f32[4,512]{1,0:T(4,128)} %pad_maximum_fusion.20.in_ref), custom_call_target="tpu_custom_call" | custom-call | tf_op jit(solution)/shard_map/pallas_call | solution.py:77
  291.1 4.5 fusion.207
  295.8 3.2 fusion.167
  299.1 3.0 fusion.174
  302.8 11.2 %shard_map.273 = f32[4,512]{1,0:T(4,128)} custom-call(f32[4,512]{1,0:T(4,128)} %pad_maximum_fusion.21.in_ref), custom_call_target="tpu_custom_call" | custom-call | tf_op jit(solution)/shard_map/pallas_call | solution.py:77
  315.4 2.2 multiply_convert_fusion.1
  318.0 2.8 add_convert_fusion
  320.8 2.4 copy.57
  324.8 4.9 pad.7
  329.7 2.1 multiply_convert_fusion.8
  332.1 1.8 add_convert_fusion.1
  335.3 3.8 bitcast_add_fusion.3
  339.2 2.5 fusion.165
  341.7 5.2 convolution_add_fusion
  348.0 2.7 bitcast_add_fusion.2
  352.0 3.8 bitcast_add_fusion.1
  355.9 1.7 fusion.89
  357.6 4.7 bitcast_add_fusion
  363.9 6.6 %convolution_add_fusion.1 = f32[3,3,512,512]{3,2,1,0:T(8,128)} fusion(f32[3,3,512,512]{3,2,1,0:T(8,128)S(1)} %fusion.163, bf16[4,7,7,512]{3,0,2,1:T(4,128)(2,1)S(1)} %multiply_convert_fusion.14, bf16[4,14,14,512]{3,2,1,0:T(8,128)(2,1)S(1)} %copy-done.62), kind=kOutput, calls=%fused_computation.14 | convolution fusion | flops 841220096 | bytes 19877888 | tf_op jit(solution)/shard_map/conv_general_dilated | solution.py:479
  371.8 2.3 fusion.8
  374.1 2.9 copy.55
  377.1 183.8 %shard_map.274 = (f32[64,2048]{1,0:T(8,128)}, f32[576,512]{1,0:T(8,128)}, f32[256,512]{1,0:T(8,128)}, f32[64,2048]{1,0:T(8,128)}, f32[128,2048]{1,0:T(8,128)}, /*index=5*/f32[576,512]{1,0:T(8,128)}, f32[128,512]{1,0:T(8,128)}) custom-call(f32[2,2,2,64,2048]{4,3,2,1,0:T(8,128)} %bitcast.319, f32[2,2,2,576,512]{4,3,2,1,0:T(8,128)} %bitcast.302, ...), custom_call_target="tpu_custom_call" | custom-call | tf_op jit(solution)/shard_map/pallas_call | solution.py:420
  563.5 1.8 copy.165
  565.2 2.4 copy.166
  (446 shorter events, 56.2 us)
Async XLA Ops:
  0.6 84.1 %copy-start = (bf16[2048,512]{1,0:T(8,128)(2,1)S(1)}, bf16[2048,512]{1,0:T(8,128)(2,1)}, u32[]{:S(2)}) copy-start(bf16[2048,512]{1,0:T(8,128)(2,1)} %param.21) | copy-start | bytes 6291460
  1.6 83.6 %copy-start.87 = (f32[1,2048]{1,0:T(1,128)}, f32[1,2048]{1,0:T(1,128)S(1)}, u32[]{:S(2)}) copy-start(f32[1,2048]{1,0:T(1,128)S(1)} %get-tuple-element.145) | copy-start | bytes 24580
  1.6 83.6 %copy-start.89 = (f32[1,2048]{1,0:T(1,128)}, f32[1,2048]{1,0:T(1,128)S(1)}, u32[]{:S(2)}) copy-start(f32[1,2048]{1,0:T(1,128)S(1)} %get-tuple-element.146) | copy-start | bytes 24580
  2.6 82.7 %copy-start.111 = (f32[1,2048]{1,0:T(1,128)}, f32[1,2048]{1,0:T(1,128)S(1)}, u32[]{:S(2)}) copy-start(f32[1,2048]{1,0:T(1,128)S(1)} %get-tuple-element.148) | copy-start | bytes 24580
  2.6 82.7 %copy-start.113 = (f32[1,2048]{1,0:T(1,128)}, f32[1,2048]{1,0:T(1,128)S(1)}, u32[]{:S(2)}) copy-start(f32[1,2048]{1,0:T(1,128)S(1)} %get-tuple-element.149) | copy-start | bytes 24580
  8.7 22.0 %copy-start.155 = (f32[1,512]{1,0:T(1,128)}, f32[1,512]{1,0:T(1,128)S(1)}, u32[]{:S(2)}) copy-start(f32[1,512]{1,0:T(1,128)S(1)} %get-tuple-element.206) | copy-start | bytes 6148
  8.7 47.3 %copy-start.98 = (f32[1,512]{1,0:T(1,128)}, f32[1,512]{1,0:T(1,128)S(1)}, u32[]{:S(2)}) copy-start(f32[1,512]{1,0:T(1,128)S(1)} %get-tuple-element.205) | copy-start | bytes 6148
  8.7 169.3 %copy-start.100 = (f32[1,512]{1,0:T(1,128)}, f32[1,512]{1,0:T(1,128)S(1)}, u32[]{:S(2)}) copy-start(f32[1,512]{1,0:T(1,128)S(1)} %get-tuple-element.204) | copy-start | bytes 6148
  8.8 22.0 %copy-start.149 = (f32[1,512]{1,0:T(1,128)}, f32[1,512]{1,0:T(1,128)S(1)}, u32[]{:S(2)}) copy-start(f32[1,512]{1,0:T(1,128)S(1)} %get-tuple-element.202) | copy-start | bytes 6148
  8.8 47.3 %copy-start.91 = (f32[1,512]{1,0:T(1,128)}, f32[1,512]{1,0:T(1,128)S(1)}, u32[]{:S(2)}) copy-start(f32[1,512]{1,0:T(1,128)S(1)} %get-tuple-element.201) | copy-start | bytes 6148
  8.8 169.2 %copy-start.93 = (f32[1,512]{1,0:T(1,128)}, f32[1,512]{1,0:T(1,128)S(1)}, u32[]{:S(2)}) copy-start(f32[1,512]{1,0:T(1,128)S(1)} %get-tuple-element.200) | copy-start | bytes 6148
  30.7 17.5 %copy-start.46 = (f32[16,3,3,512]{3,0,2,1:T(8,128)}, f32[16,3,3,512]{3,0,2,1:T(8,128)S(1)}, u32[]{:S(2)}) copy-start(f32[16,3,3,512]{3,0,2,1:T(8,128)S(1)} %get-tuple-element.241) | copy-start | bytes 884740
  34.7 21.3 %copy-start.33 = (f32[4,7,7,512]{3,0,2,1:T(4,128)}, f32[4,7,7,512]{3,0,2,1:T(4,128)S(1)}, u32[]{:S(2)}) copy-start(f32[4,7,7,512]{3,0,2,1:T(4,128)S(1)} %get-tuple-element.242) | copy-start | bytes 1204228
  47.6 8.5 %copy-start.129 = (f32[1,512]{1,0:T(1,128)}, f32[1,512]{1,0:T(1,128)S(1)}, u32[]{:S(2)}) copy-start(f32[1,512]{1,0:T(1,128)S(1)} %get-tuple-element.208) | copy-start | bytes 6148
  48.2 7.9 %copy-start.134 = (f32[512]{0:T(512)}, f32[512]{0:T(512)S(1)}, u32[]{:S(2)}) copy-start(f32[512]{0:T(512)S(1)} %get-tuple-element.232) | copy-start | bytes 6148
  112.1 65.9 %copy-start.35 = (f32[4,7,7,512]{3,0,2,1:T(4,128)}, f32[4,7,7,512]{3,0,2,1:T(4,128)S(1)}, u32[]{:S(2)}) copy-start(f32[4,7,7,512]{3,0,2,1:T(4,128)S(1)} %get-tuple-element.249) | copy-start | bytes 1204228
  124.4 53.7 %copy-start.131 = (f32[1,512]{1,0:T(1,128)}, f32[1,512]{1,0:T(1,128)S(1)}, u32[]{:S(2)}) copy-start(f32[1,512]{1,0:T(1,128)S(1)} %get-tuple-element.192) | copy-start | bytes 6148
  125.0 53.1 %copy-start.136 = (f32[512]{0:T(512)}, f32[512]{0:T(512)S(1)}, u32[]{:S(2)}) copy-start(f32[512]{0:T(512)S(1)} %get-tuple-element.236) | copy-start | bytes 6148
  147.6 7.1 %copy-start.67 = (bf16[16,3,3,2048]{3,0,2,1:T(8,128)(2,1)S(1)}, bf16[16,3,3,2048]{3,0,2,1:T(8,128)(2,1)}, u32[]{:S(2)}) copy-start(bf16[16,3,3,2048]{3,0,2,1:T(8,128)(2,1)} %param.29) | copy-start | bytes 1769476
  180.4 22.4 %slice-start = ((s8[4718592]{0:T(1024)(128)(4,1)}), s8[524288]{0:T(1024)(128)(4,1)S(1)}, s32[]{:S(2)}) async-start(s8[4718592]{0:T(1024)(128)(4,1)} %bitcast.306), calls=%async_computation | async-start | bytes 1048576
  196.7 5.9 %copy-start.81 = (bf16[4,7,7,512]{3,0,2,1:T(4,128)(2,1)}, bf16[4,7,7,512]{3,0,2,1:T(4,128)(2,1)S(1)}, u32[]{:S(2)}) copy-start(bf16[4,7,7,512]{3,0,2,1:T(4,128)(2,1)S(1)} %multiply_convert_fusion.16) | copy-start | bytes 602116
  196.7 5.9 %copy-start.37 = (f32[16,3,3,512]{3,0,2,1:T(8,128)S(1)}, f32[16,3,3,512]{3,0,2,1:T(8,128)}, u32[]{:S(2)}) copy-start(f32[16,3,3,512]{3,0,2,1:T(8,128)} %get-tuple-element.248) | copy-start | bytes 884740
  196.7 5.9 %copy-start.76 = (f32[16,3,3,512]{3,0,2,1:T(8,128)S(1)}, f32[16,3,3,512]{3,0,2,1:T(8,128)}, u32[]{:S(2)}) copy-start(f32[16,3,3,512]{3,0,2,1:T(8,128)} %get-tuple-element.252) | copy-start | bytes 884740
  196.7 5.9 %copy-start.120 = (f32[1,512]{1,0:T(1,128)S(1)}, f32[1,512]{1,0:T(1,128)}, u32[]{:S(2)}) copy-start(f32[1,512]{1,0:T(1,128)} %copy-done.118) | copy-start | bytes 6148
  196.7 6.0 %slice-start.1 = ((s8[4718592]{0:T(1024)(128)(4,1)}), s8[4194304]{0:T(1024)(128)(4,1)S(1)}, s32[]{:S(2)}) async-start(s8[4718592]{0:T(1024)(128)(4,1)} %bitcast.306), calls=%async_computation.1 | async-start | bytes 8388608
  219.6 6.4 %copy-start.79 = (bf16[4,7,7,512]{3,0,2,1:T(4,128)(2,1)}, bf16[4,7,7,512]{3,0,2,1:T(4,128)(2,1)S(1)}, u32[]{:S(2)}) copy-start(bf16[4,7,7,512]{3,0,2,1:T(4,128)(2,1)S(1)} %multiply_convert_fusion.15) | copy-start | bytes 602116
  219.6 6.4 %copy-start.54 = (f32[16,3,3,512]{3,0,2,1:T(8,128)S(1)}, f32[16,3,3,512]{3,0,2,1:T(8,128)}, u32[]{:S(2)}) copy-start(f32[16,3,3,512]{3,0,2,1:T(8,128)} %get-tuple-element.104) | copy-start | bytes 884740
  219.6 6.4 %copy-start.167 = (f32[512]{0:T(512)S(1)}, f32[512]{0:T(512)}, u32[]{:S(2)}) copy-start(f32[512]{0:T(512)} %get-tuple-element.224) | copy-start | bytes 6148
  219.6 6.5 %copy-start.6 = (f32[16,3,3,2048]{3,0,2,1:T(8,128)S(1)}, f32[16,3,3,2048]{3,0,2,1:T(8,128)}, u32[]{:S(2)}) copy-start(f32[16,3,3,2048]{3,0,2,1:T(8,128)} %get-tuple-element.243) | copy-start | bytes 3538948
  219.7 6.5 %copy-start.10 = (f32[16,3,3,2048]{3,0,2,1:T(8,128)S(1)}, f32[16,3,3,2048]{3,0,2,1:T(8,128)}, u32[]{:S(2)}) copy-start(f32[16,3,3,2048]{3,0,2,1:T(8,128)} %get-tuple-element.238) | copy-start | bytes 3538948
  219.7 6.5 %copy-start.25 = (f32[16,3,3,2048]{3,0,2,1:T(8,128)S(1)}, f32[16,3,3,2048]{3,0,2,1:T(8,128)}, u32[]{:S(2)}) copy-start(f32[16,3,3,2048]{3,0,2,1:T(8,128)} %get-tuple-element.107) | copy-start | bytes 3538948
  219.7 6.5 %copy-start.88 = (f32[1,2048]{1,0:T(1,128)S(1)}, f32[1,2048]{1,0:T(1,128)}, u32[]{:S(2)}) copy-start(f32[1,2048]{1,0:T(1,128)} %copy-done.87) | copy-start | bytes 24580
  219.7 6.5 %copy-start.90 = (f32[1,2048]{1,0:T(1,128)S(1)}, f32[1,2048]{1,0:T(1,128)}, u32[]{:S(2)}) copy-start(f32[1,2048]{1,0:T(1,128)} %copy-done.89) | copy-start | bytes 24580
  219.7 6.5 %copy-start.104 = (f32[2048]{0:T(1024)S(1)}, f32[2048]{0:T(1024)}, u32[]{:S(2)}) copy-start(f32[2048]{0:T(1024)} %copy-done.103) | copy-start | bytes 24580
  219.7 6.5 %copy-start.106 = (f32[2048]{0:T(1024)S(1)}, f32[2048]{0:T(1024)}, u32[]{:S(2)}) copy-start(f32[2048]{0:T(1024)} %copy-done.105) | copy-start | bytes 24580
  219.7 6.5 %copy-start.112 = (f32[1,2048]{1,0:T(1,128)S(1)}, f32[1,2048]{1,0:T(1,128)}, u32[]{:S(2)}) copy-start(f32[1,2048]{1,0:T(1,128)} %copy-done.111) | copy-start | bytes 24580
  219.7 6.5 %copy-start.114 = (f32[1,2048]{1,0:T(1,128)S(1)}, f32[1,2048]{1,0:T(1,128)}, u32[]{:S(2)}) copy-start(f32[1,2048]{1,0:T(1,128)} %copy-done.113) | copy-start | bytes 24580
  226.2 25.6 %copy-start.108 = (f32[2048]{0:T(1024)S(1)}, f32[2048]{0:T(1024)}, u32[]{:S(2)}) copy-start(f32[2048]{0:T(1024)} %copy-done.107) | copy-start | bytes 24580
  226.3 25.6 %copy-start.110 = (f32[2048]{0:T(1024)S(1)}, f32[2048]{0:T(1024)}, u32[]{:S(2)}) copy-start(f32[2048]{0:T(1024)} %copy-done.109) | copy-start | bytes 24580
  226.3 25.6 %copy-start.139 = (f32[2048]{0:T(1024)S(1)}, f32[2048]{0:T(1024)}, u32[]{:S(2)}) copy-start(f32[2048]{0:T(1024)} %get-tuple-element.187) | copy-start | bytes 24580
  226.3 25.6 %copy-start.140 = (f32[2048]{0:T(1024)S(1)}, f32[2048]{0:T(1024)}, u32[]{:S(2)}) copy-start(f32[2048]{0:T(1024)} %get-tuple-element.189) | copy-start | bytes 24580
  275.6 15.3 %copy-start.45 = (f32[4,7,7,512]{3,0,2,1:T(4,128)S(1)}, f32[4,7,7,512]{3,0,2,1:T(4,128)}, u32[]{:S(2)}) copy-start(f32[4,7,7,512]{3,0,2,1:T(4,128)} %get-tuple-element.100) | copy-start | bytes 1204228
  275.6 15.3 %copy-start.164 = (f32[512]{0:T(512)S(1)}, f32[512]{0:T(512)}, u32[]{:S(2)}) copy-start(f32[512]{0:T(512)} %get-tuple-element.233) | copy-start | bytes 6148
  275.6 23.5 %slice-start.4 = ((s8[4718592]{0:T(1024)(128)(4,1)}), s8[524288]{0:T(1024)(128)(4,1)S(1)}, s32[]{:S(2)}) async-start(s8[4718592]{0:T(1024)(128)(4,1)} %bitcast.316), calls=%async_computation.4 | async-start | bytes 1048576
  291.1 7.9 %slice-start.5 = ((s8[4718592]{0:T(1024)(128)(4,1)}), s8[4194304]{0:T(1024)(128)(4,1)S(1)}, s32[]{:S(2)}) async-start(s8[4718592]{0:T(1024)(128)(4,1)} %bitcast.316), calls=%async_computation.5 | async-start | bytes 8388608
  299.1 16.3 %copy-start.162 = (f32[512]{0:T(512)S(1)}, f32[512]{0:T(512)}, u32[]{:S(2)}) copy-start(f32[512]{0:T(512)} %get-tuple-element.231) | copy-start | bytes 6148
  324.8 7.0 %copy-start.30 = (bf16[1024,512]{1,0:T(8,128)(2,1)S(1)}, bf16[1024,512]{1,0:T(8,128)(2,1)}, u32[]{:S(2)}) copy-start(bf16[1024,512]{1,0:T(8,128)(2,1)} %param.17) | copy-start | bytes 3145732
  363.8 6.6 %copy-start.19 = (bf16[4,14,14,512]{3,2,1,0:T(8,128)(2,1)S(1)}, bf16[4,14,14,512]{3,2,1,0:T(8,128)(2,1)}, u32[]{:S(2)}) copy-start(bf16[4,14,14,512]{3,2,1,0:T(8,128)(2,1)} %copy-done.18) | copy-start | bytes 2408452
  363.8 6.6 %copy-start.97 = (bf16[4,14,14,1024]{3,0,2,1:T(4,128)(2,1)S(1)}, bf16[4,14,14,1024]{3,0,2,1:T(4,128)(2,1)}, u32[]{:S(2)}) copy-start(bf16[4,14,14,1024]{3,0,2,1:T(4,128)(2,1)} %param.15) | copy-start | bytes 4816900
  377.0 183.9 %copy-start.172 = (f32[1,512]{1,0:T(1,128)S(1)}, f32[1,512]{1,0:T(1,128)}, u32[]{:S(2)}) copy-start(f32[1,512]{1,0:T(1,128)} %get-tuple-element.181) | copy-start | bytes 6148
  377.0 183.9 %copy-start.174 = (f32[1,512]{1,0:T(1,128)S(1)}, f32[1,512]{1,0:T(1,128)}, u32[]{:S(2)}) copy-start(f32[1,512]{1,0:T(1,128)} %get-tuple-element.175) | copy-start | bytes 6148
  377.0 183.9 %copy-start.176 = (f32[1,512]{1,0:T(1,128)S(1)}, f32[1,512]{1,0:T(1,128)}, u32[]{:S(2)}) copy-start(f32[1,512]{1,0:T(1,128)} %get-tuple-element.169) | copy-start | bytes 6148
  377.0 183.9 %copy-start.178 = (f32[1,512]{1,0:T(1,128)S(1)}, f32[1,512]{1,0:T(1,128)}, u32[]{:S(2)}) copy-start(f32[1,512]{1,0:T(1,128)} %get-tuple-element.163) | copy-start | bytes 6148
  377.0 184.6 %copy-start.171 = (f32[1,512]{1,0:T(1,128)S(1)}, f32[1,512]{1,0:T(1,128)}, u32[]{:S(2)}) copy-start(f32[1,512]{1,0:T(1,128)} %get-tuple-element.180) | copy-start | bytes 6148
  377.0 184.6 %copy-start.173 = (f32[1,512]{1,0:T(1,128)S(1)}, f32[1,512]{1,0:T(1,128)}, u32[]{:S(2)}) copy-start(f32[1,512]{1,0:T(1,128)} %get-tuple-element.174) | copy-start | bytes 6148
  377.0 184.5 %copy-start.175 = (f32[1,512]{1,0:T(1,128)S(1)}, f32[1,512]{1,0:T(1,128)}, u32[]{:S(2)}) copy-start(f32[1,512]{1,0:T(1,128)} %get-tuple-element.168) | copy-start | bytes 6148
  377.0 184.5 %copy-start.177 = (f32[1,512]{1,0:T(1,128)S(1)}, f32[1,512]{1,0:T(1,128)}, u32[]{:S(2)}) copy-start(f32[1,512]{1,0:T(1,128)} %get-tuple-element.162) | copy-start | bytes 6148
  377.0 185.1 %copy-start.142 = (f32[1,2048]{1,0:T(1,128)S(1)}, f32[1,2048]{1,0:T(1,128)}, u32[]{:S(2)}) copy-start(f32[1,2048]{1,0:T(1,128)} %get-tuple-element.135) | copy-start | bytes 24580
  377.0 185.1 %copy-start.145 = (f32[1,2048]{1,0:T(1,128)S(1)}, f32[1,2048]{1,0:T(1,128)}, u32[]{:S(2)}) copy-start(f32[1,2048]{1,0:T(1,128)} %get-tuple-element.115) | copy-start | bytes 24580
  377.1 185.1 %copy-start.146 = (f32[1,2048]{1,0:T(1,128)S(1)}, f32[1,2048]{1,0:T(1,128)}, u32[]{:S(2)}) copy-start(f32[1,2048]{1,0:T(1,128)} %get-tuple-element.117) | copy-start | bytes 24580
  377.1 185.8 %copy-start.141 = (f32[1,2048]{1,0:T(1,128)S(1)}, f32[1,2048]{1,0:T(1,128)}, u32[]{:S(2)}) copy-start(f32[1,2048]{1,0:T(1,128)} %get-tuple-element.134) | copy-start | bytes 24580
  377.1 185.8 %copy-start.143 = (f32[1,2048]{1,0:T(1,128)S(1)}, f32[1,2048]{1,0:T(1,128)}, u32[]{:S(2)}) copy-start(f32[1,2048]{1,0:T(1,128)} %get-tuple-element.114) | copy-start | bytes 24580
  377.1 185.7 %copy-start.144 = (f32[1,2048]{1,0:T(1,128)S(1)}, f32[1,2048]{1,0:T(1,128)}, u32[]{:S(2)}) copy-start(f32[1,2048]{1,0:T(1,128)} %get-tuple-element.116) | copy-start | bytes 24580
  560.9 6.7 %copy-start.72 = (f32[64,2048]{1,0:T(8,128)S(1)}, f32[64,2048]{1,0:T(8,128)}, u32[]{:S(2)}) copy-start(f32[64,2048]{1,0:T(8,128)} %get-tuple-element.281) | copy-start | bytes 1572868
  (121 other events, 380.4 us)

commit v2 on v1

v2 whole, which is shorter than its diff:
```python
import functools
import math

import jax
import jax.numpy as jnp
from jax import lax
from jax.experimental import pallas as pl
from jax.experimental.pallas import tpu as pltpu
from jax.sharding import PartitionSpec as P

EPS = 1e-05
MESH_ID = pl.DeviceIdType.MESH


PANEL = 512
DEPTH = 8


def chunk_list(shapes, dp_size, half):
    chunks = []
    for number, (rows, columns) in enumerate(shapes):
        own = rows // dp_size
        for panel in range(columns // PANEL):
            for start in range(0, own, 2 * half):
                chunks.append((number, start, panel * PANEL))
    return chunks


class Reducer:
    def __init__(self, sizes, shapes, half, weights, outs, scratch):
        dp_size, grp_size = sizes
        self.half = half
        self.weights = weights
        self.outs = outs
        (
            self.acc,
            self.rc,
            self.rd,
            self.fin,
            self.load_sem,
            self.out_sem,
            self.send_sem,
            self.recv_sem,
            self.credit,
        ) = scratch
        self.chunks = chunk_list(shapes, dp_size, half)
        self.dp = lax.axis_index("dp")
        self.grp = lax.axis_index("grp")
        x_bits, dp_bits, y_bits = bit_counts(sizes)
        self.x_bits, self.dp_bits = x_bits, dp_bits
        self.orders = axis_orders(sizes)
        self.steps = x_bits + dp_bits
        self.lanes = len(self.orders)
        self.groups = -(-len(self.chunks) // self.lanes)
        self.stages = self.steps + x_bits + 3
        self.slots = self.lanes * (self.steps + 2)

    def bit(self, step):
        kind, index = step
        return ((self.grp >> (index + 1)) & 1) if kind == "x" else ((self.dp >> index) & 1)

    def partner(self, step):
        kind, index = step
        if kind == "x":
            return (self.dp, self.grp ^ (2 << index))
        return (self.dp ^ (1 << index), self.grp)

    def sibling(self):
        return (self.dp, self.grp ^ 1)

    def region(self, done, last_flip):
        place = [slice(None)] * self.dp_bits
        width = PANEL
        column = 0
        for number, step in enumerate(done):
            bit = self.bit(step)
            if last_flip and number == len(done) - 1:
                bit = 1 - bit
            if step[0] == "d":
                place[self.dp_bits - 1 - step[1]] = bit
            else:
                width = width // 2
                column = column + bit * width
        return place, column, width

    def view(self, ref, slot, done, flip=False):
        place, column, width = self.region(done, flip)
        if isinstance(column, int):
            cols = pl.ds(column, width)
        else:
            cols = pl.ds(pl.multiple_of(column, width), width)
        return ref.at[(slot, *place, slice(None), cols)]

    def landing(self, k, order, count):
        return self.rd[k % self.lanes][count - 1].at[(k // self.lanes) % 2]

    def c_copy(self, k, slot):
        number, start, column = self.chunks[k]
        source = self.weights[number].at[
            (slice(None),) * self.dp_bits
            + (
                pl.ds(start + (1 - self.grp % 2) * self.half, self.half),
                pl.ds(column, PANEL),
            )
        ]
        return pltpu.make_async_remote_copy(
            src_ref=source,
            dst_ref=self.rc.at[k % (2 * self.lanes)],
            send_sem=self.send_sem.at[slot, 0],
            recv_sem=self.recv_sem.at[slot, 0],
            device_id=self.sibling(),
            device_id_type=MESH_ID,
        )

    def load(self, k, slot):
        number, start, column = self.chunks[k]
        source = self.weights[number].at[
            (slice(None),) * self.dp_bits
            + (pl.ds(start + (self.grp % 2) * self.half, self.half), pl.ds(column, PANEL))
        ]
        return pltpu.make_async_copy(source, self.acc.at[slot], self.load_sem.at[slot])

    def d_copy(self, k, slot, count):
        order = self.orders[k % self.lanes]
        return pltpu.make_async_remote_copy(
            src_ref=self.view(self.acc, slot, order[:count], True),
            dst_ref=self.landing(k, order, count),
            send_sem=self.send_sem.at[slot, count],
            recv_sem=self.recv_sem.at[slot, count],
            device_id=self.partner(order[count - 1]),
            device_id_type=MESH_ID,
        )

    def x_columns(self, count):
        steps = [("x", i) for i in range(self.x_bits - count)]
        place, column, width = self.region(steps, False)
        if isinstance(column, int):
            return pl.ds(column, width)
        return pl.ds(pl.multiple_of(column, width), width)

    def ag_copy(self, k, slot, count):
        columns = self.x_columns(count)
        block = self.fin.at[slot, :, columns]
        stage = self.steps + 1 + count
        return pltpu.make_async_remote_copy(
            src_ref=block,
            dst_ref=block,
            send_sem=self.send_sem.at[slot, stage],
            recv_sem=self.recv_sem.at[slot, stage],
            device_id=self.partner(("x", self.x_bits - 1 - count)),
            device_id_type=MESH_ID,
        )

    def out_block(self, k):
        number, start, column = self.chunks[k]
        return self.outs[number].at[
            pl.ds(start + (self.grp % 2) * self.half, self.half), pl.ds(column, PANEL)
        ]

    def out_copies(self, k, slot):
        stage = self.stages - 2
        remote = pltpu.make_async_remote_copy(
            src_ref=self.fin.at[slot],
            dst_ref=self.out_block(k),
            send_sem=self.send_sem.at[slot, stage],
            recv_sem=self.recv_sem.at[slot, stage],
            device_id=self.sibling(),
            device_id_type=MESH_ID,
        )
        local = pltpu.make_async_copy(self.fin.at[slot], self.out_block(k), self.out_sem.at[slot])
        return remote, local

    def period(self, stage):
        return 2 * self.lanes if stage <= self.steps else self.slots

    def give(self, k, stage, device):
        period = self.period(stage)
        if k + period < len(self.chunks):
            pl.semaphore_signal(
                self.credit.at[k % period, stage],
                inc=1,
                device_id=device,
                device_id_type=MESH_ID,
            )

    def take(self, k, stage):
        period = self.period(stage)
        if k >= period:
            pl.semaphore_wait(self.credit.at[k % period, stage], 1)

    def add(self, k, slot, order, count, target=None):
        done = order[:count]
        place, column, width = self.region(done, False)
        free = [number for number, value in enumerate(place) if isinstance(value, slice)]
        cols = pl.ds(column, width)
        if not isinstance(column, int):
            cols = pl.ds(pl.multiple_of(column, width), width)

        def one(index, carry):
            where = list(place)
            lead = []
            for position, axis in enumerate(free):
                value = (index >> (len(free) - 1 - position)) & 1
                where[axis] = value
                lead.append(value)
            if count == 0:
                arrived = self.rc[(k % (2 * self.lanes), *lead)]
            else:
                arrived = self.rd[k % self.lanes][count - 1][((k // self.lanes) % 2, *lead)]
            here = (slot, *where, slice(None), cols)
            if target is None:
                self.acc[here] = self.acc[here] + arrived
            else:
                self.fin[slot, :, self.x_columns(0)] = self.acc[here] + arrived
            return carry

        total = 2 ** len(free)
        if total == 1:
            one(0, 0)
        else:
            lax.fori_loop(0, total, one, 0)

    def run(self, k, stage):
        slot = k % self.slots
        order = self.orders[k % self.lanes]
        steps = self.steps
        if stage == 0:
            self.load(k, slot).start()
            self.take(k, 0)
            self.c_copy(k, slot).start()
        elif stage <= steps + 1:
            count = stage - 1
            if count == 0:
                self.load(k, slot).wait()
                self.c_copy(k, slot).wait()
            else:
                self.d_copy(k, slot, count).wait()
            self.add(k, slot, order, count, None if count < steps else True)
            device = self.sibling() if count == 0 else self.partner(order[count - 1])
            self.give(k, count, device)
            self.take(k, count + 1)
            if count < steps:
                self.d_copy(k, slot, count + 1).start()
            else:
                self.ag_copy(k, slot, 0).start()
        elif stage <= steps + self.x_bits:
            count = stage - steps - 1
            self.ag_copy(k, slot, count - 1).wait()
            self.take(k, stage)
            self.ag_copy(k, slot, count).start()
        elif stage == self.stages - 2:
            self.ag_copy(k, slot, self.x_bits - 1).wait()
            remote, local = self.out_copies(k, slot)
            remote.start()
            local.start()
        else:
            remote, local = self.out_copies(k, slot)
            remote.wait()
            local.wait()
            for count in range(self.x_bits):
                device = self.partner(("x", self.x_bits - 1 - count))
                self.give(k, steps + 1 + count, device)

    def step(self, time):
        for stage in reversed(range(self.stages)):
            group = time - stage
            if 0 <= group < self.groups:
                for k in range(
                    self.lanes * group, min(self.lanes * (group + 1), len(self.chunks))
                ):
                    self.run(k, stage)


def bit_counts(sizes):
    dp_size, grp_size = sizes
    x_bits = (grp_size // 2).bit_length() - 1
    dp_bits = dp_size.bit_length() - 1
    return x_bits, dp_bits, x_bits


def axis_orders(sizes):
    x_bits, dp_bits, y_bits = bit_counts(sizes)
    xs = [("x", i) for i in range(x_bits)]
    ys = [("d", i) for i in range(y_bits)]
    zs = [("d", i) for i in range(y_bits, dp_bits)]
    orders = [xs + ys + zs, ys + zs[:1] + xs + zs[1:], zs[:1] + ys + xs + zs[1:]]
    return orders if x_bits + dp_bits < 5 else orders[:2]


def reducer_scratch(sizes, half):
    x_bits, dp_bits, _ = bit_counts(sizes)
    steps = x_bits + dp_bits
    groups = steps + 2
    orders = axis_orders(sizes)
    slots = len(orders) * groups
    stages = steps + x_bits + 3
    landings = []
    for order in orders:
        for count in range(1, steps + 1):
            done = [step[0] for step in order[:count]]
            lead = (2,) * (dp_bits - done.count("d"))
            width = PANEL >> done.count("x")
            landings.append(pltpu.VMEM((2,) + lead + (half, width), jnp.float32))
    block = (slots,) + (2,) * dp_bits + (half, PANEL)
    return [
        pltpu.VMEM(block, jnp.float32),
        pltpu.VMEM((2 * len(orders),) + block[1:], jnp.float32),
        *landings,
        pltpu.VMEM((slots, half, PANEL), jnp.float32),
        pltpu.SemaphoreType.DMA((slots,)),
        pltpu.SemaphoreType.DMA((slots,)),
        pltpu.SemaphoreType.DMA((slots, stages)),
        pltpu.SemaphoreType.DMA((slots, stages)),
        pltpu.SemaphoreType.REGULAR((slots, stages)),
    ]


C0 = math.sqrt(2.0 / math.pi)
C1 = C0 * 0.044715
W = 512
BLK = 16
FIRST, SECOND, THIRD, SIDE, FOURTH, FIFTH, SIXTH = 0, 1, 2, 6, 10, 11, 12


def gelu(u):
    t = jnp.tanh(u * (C0 + C1 * u * u))
    return u * (0.5 + 0.5 * t)


def gelu_both(u):
    square = u * u
    t = jnp.tanh(u * (C0 + C1 * square))
    half = 0.5 + 0.5 * t
    slope = half + 0.5 * u * (1.0 - t * t) * (C0 + 3.0 * C1 * square)
    return u * half, slope


def dot(a, b):
    return lax.dot_general(a, b, (((1,), (0,)), ((), ())), preferred_element_type=jnp.float32)


def dot_t(a, b):
    return lax.dot_general(a, b, (((1,), (1,)), ((), ())), preferred_element_type=jnp.float32)


def dot_rows(a, b):
    return lax.dot_general(a, b, (((0,), (0,)), ((), ())), preferred_element_type=jnp.float32)


class Exchange:
    def __init__(self, sizes, refs):
        self.dp_size, self.grp_size = sizes
        self.msg, self.gbuf, self.part, self.dbuf, self.tot, self.send, self.recv = refs
        self.dp = lax.axis_index("dp")
        self.grp = lax.axis_index("grp")
        self.turn = 1

    def copy(self, phase, k, source, target, device):
        result = pltpu.make_async_remote_copy(
            src_ref=source,
            dst_ref=target,
            send_sem=self.send.at[self.turn, phase, k],
            recv_sem=self.recv.at[self.turn, phase, k],
            device_id=device,
            device_id_type=MESH_ID,
        )
        result.start()
        self.copies.append(result)

    def begin(self):
        self.turn = 1 - self.turn
        return self.msg.at[self.turn]

    def start(self, pieces):
        turn = self.turn
        self.cut = pieces % self.grp_size == 0
        self.own = pieces // self.grp_size if self.cut else pieces
        own = self.own
        self.copies = []
        for k in range(1, self.grp_size):
            peer = self.grp ^ k
            first = peer * own if self.cut else 0
            self.copy(
                0,
                k,
                self.msg.at[turn, pl.ds(first, own)],
                self.gbuf.at[turn, self.grp, pl.ds(0, own)],
                (self.dp, peer),
            )
        for q in range(own):
            here = self.grp * own + q if self.cut else q
            self.gbuf[turn, self.grp, q] = self.msg[turn, here]

    def wait(self):
        for copy in self.copies:
            copy.wait()
        self.copies = []

    def middle(self):
        turn = self.turn
        self.wait()
        for q in range(self.own):
            total = self.gbuf[turn, 0, q]
            for k in range(1, self.grp_size):
                total = total + self.gbuf[turn, k, q]
            self.part[turn, q] = total
            self.dbuf[turn, self.dp, q] = total
        for k in range(1, self.dp_size):
            self.copy(
                1,
                k,
                self.part.at[turn, pl.ds(0, self.own)],
                self.dbuf.at[turn, self.dp, pl.ds(0, self.own)],
                (self.dp ^ k, self.grp),
            )

    def last(self):
        turn = self.turn
        self.wait()
        for q in range(self.own):
            total = self.dbuf[turn, 0, q]
            for k in range(1, self.dp_size):
                total = total + self.dbuf[turn, k, q]
            here = self.grp * self.own + q if self.cut else q
            self.tot[turn, here] = total
        if self.cut:
            block = self.tot.at[turn, pl.ds(self.grp * self.own, self.own)]
            for k in range(1, self.grp_size):
                self.copy(2, k, block, block, (self.dp, self.grp ^ k))

    def finish(self):
        self.wait()
        return self.tot.at[self.turn]


class Net:
    def __init__(self, sizes, geometry, refs):
        self.sizes = sizes
        self.devices = sizes[0] * sizes[1]
        self.crops, self.per = geometry
        self.top = self.crops * 64
        self.rows = self.top + 9 * self.per
        self.top_blocks = self.top // BLK
        self.blocks = self.rows // BLK
        for name, ref in refs.items():
            setattr(self, name, ref)
        self.slot = 0
        self.pending = [[], []]


    def load(self, number, source, target):
        copy = pltpu.make_async_copy(source, target, self.load_sem.at[number])
        copy.start()
        return copy


    def sweep(self, body, init):
        results = []
        for group in range(2):
            low, high = (0, self.top_blocks) if group == 0 else (self.top_blocks, self.blocks)

            def one(index, carry, group=group):
                rows = pl.ds(pl.multiple_of(index * BLK, BLK), BLK)
                return body(group, index, rows, self.keeper(group, index), carry)

            results.append(lax.fori_loop(low, high, one, init))
        return results

    def keeper(self, group, index):
        if group == 1:
            return lambda value: value
        row = index * BLK + lax.broadcasted_iota(jnp.int32, (BLK, 128), 0)
        valid = ((row & 7) != 7) & ((row & 63) < 56)
        valid = jnp.concatenate([valid.astype(jnp.float32)] * (W // 128), axis=1)
        return lambda value: value * valid

    def zeros(self):
        return jnp.zeros((8, W), jnp.float32)

    @staticmethod
    def fold(value):
        return value[0:8] + value[8:16]

    def put(self, msg, piece, results, second=0):
        for group in range(2):
            first, other = results[group][0], results[group][1 + second]
            msg[piece, pl.ds(2 * group, 1)] = jnp.sum(first, axis=0, keepdims=True)
            msg[piece, pl.ds(2 * group + 1, 1)] = jnp.sum(other, axis=0, keepdims=True)

    def count(self, group, scale):
        pixels = (49 * self.crops, 9 * self.per)[group]
        return float(pixels * scale * self.devices)

    def moments(self, total, piece, norm, scale=1):
        for group in range(2):
            count = self.count(group, scale)
            mean = total[piece, pl.ds(2 * group, 1)] / count
            square = total[piece, pl.ds(2 * group + 1, 1)] / count
            self.mom[norm, pl.ds(2 * group, 1)] = mean
            self.mom[norm, pl.ds(2 * group + 1, 1)] = lax.rsqrt(square - mean * mean + EPS)

    def affine(self, norm, group):
        mean = self.mom[norm, pl.ds(2 * group, 1)]
        scale = self.mom[norm, pl.ds(2 * group + 1, 1)] * self.gain[norm]
        return scale, self.shift[norm] - mean * scale

    def standard(self, norm, group):
        mean = self.mom[norm, pl.ds(2 * group, 1)]
        deviation = self.mom[norm, pl.ds(2 * group + 1, 1)]
        return deviation, -mean * deviation

    def measure(self, msg, piece, source, masked, store=None):
        def body(group, index, rows, keep, carry):
            value = source[rows, :]
            if store is not None:
                store[rows, :] = value.astype(store.dtype)
            if masked:
                value = keep(value)
            total, square = carry
            return total + self.fold(value), square + self.fold(value * value)

        results = self.sweep(body, (self.zeros(), self.zeros()))
        if piece is not None:
            self.put(msg, piece, results)
        return results

    def activate(self, source, norm, target):
        params = [self.affine(norm, group) for group in range(2)]

        def body(group, index, rows, keep, carry):
            scale, offset = params[group]
            target(group, index, rows, keep(gelu(source[rows, :] * scale + offset)))
            return carry

        self.sweep(body, 0)


    def shifted(self, source, target, offset):
        start = BLK + offset
        aligned = start // 8 * 8
        skip = start - aligned

        def one(index, carry):
            rows = pl.ds(pl.multiple_of(index * BLK, BLK), BLK)
            if skip:
                value = source[pl.ds(pl.multiple_of(index * BLK + aligned, 8), 24), :]
                value = value[skip : skip + BLK]
            else:
                value = source[pl.ds(pl.multiple_of(index * BLK + aligned, 8), BLK), :]
            target[rows, :] = value.astype(jnp.bfloat16)
            return carry

        lax.fori_loop(0, self.top_blocks, one, 0)

    def moved(self, source, first, target, down, across):
        per = self.per
        for a in range(3):
            for b in range(3):
                here = pl.ds(self.top + (3 * a + b) * per, per)
                if 0 <= a + down < 3 and 0 <= b + across < 3:
                    there = pl.ds(first + (3 * (a + down) + b + across) * per, per)
                    target[here, :] = source[there, :]
                else:
                    target[here, :] = jnp.zeros((per, W), jnp.bfloat16)

    def clear_margins(self, ref):
        zero = jnp.zeros((BLK, W), jnp.float32)
        ref[pl.ds(0, BLK), :] = zero
        ref[pl.ds(BLK + self.top, BLK), :] = zero


    def norm_sums(self, msg, piece, results, norm):
        self.put(msg, piece, results)

    def back(self, norm, total, piece, second=1):
        self.dshift[norm] = total[piece, pl.ds(0, 1)] + total[piece, pl.ds(2, 1)]
        self.dgain[norm] = total[piece, pl.ds(1, 1)] + total[piece, pl.ds(3, 1)]

    def back_params(self, norm, group, total, piece, scale=1):
        count = self.count(group, scale)
        mean_grad = total[piece, pl.ds(2 * group, 1)] / count
        mean_cross = total[piece, pl.ds(2 * group + 1, 1)] / count
        factor = self.gain[norm] * self.mom[norm, pl.ds(2 * group + 1, 1)]
        return factor, mean_grad, mean_cross

    def back_sweep(self, norm, total, piece, grad, hidden, target, scale=1):
        self.back(norm, total, piece)
        params = [
            self.back_params(norm, group, total, piece, scale) + self.standard(norm, group)
            for group in range(2)
        ]

        def body(group, index, rows, keep, carry):
            factor, mean_grad, mean_cross, a, b = params[group]
            scaled = hidden[rows, :].astype(jnp.float32) * a + b
            value = factor * (grad[rows, :] - mean_grad - scaled * mean_cross)
            target(group, index, rows, keep(value))
            return carry

        self.sweep(body, 0)

    def through(self, msg, piece, norm, grad, hidden, masked):
        params = [self.affine(norm, group) + self.standard(norm, group) for group in range(2)]

        def body(group, index, rows, keep, carry):
            scale, offset, a, b = params[group]
            value = hidden[rows, :].astype(jnp.float32)
            slope = gelu_both(value * scale + offset)[1]
            result = grad[rows, :] * slope
            if masked:
                result = keep(result)
            grad[rows, :] = result
            first, cross = carry
            return first + self.fold(result), cross + self.fold(result * (value * a + b))

        results = self.sweep(body, (self.zeros(), self.zeros()))
        if piece is not None:
            self.put(msg, piece, results)
        return results


    def emit(self, number, row, column, value):
        slot = self.slot
        self.slot = 1 - slot
        self.drain(slot)
        self.stage[slot] = value
        grads = self.grads[number]
        own = grads.shape[-2]
        bits = len(grads.shape) - 2
        place = row
        while place < row + W:
            owner = place // own
            size = min(own - place % own, row + W - place)
            index = tuple((owner >> (bits - 1 - i)) & 1 for i in range(bits))
            copy = pltpu.make_async_copy(
                self.stage.at[slot, pl.ds(place - row, size)],
                grads.at[index + (pl.ds(place % own, size), pl.ds(column, W))],
                self.stage_sem.at[slot, len(self.pending[slot])],
            )
            copy.start()
            self.pending[slot].append(copy)
            place += size

    def drain(self, slot):
        for copy in self.pending[slot]:
            copy.wait()
        self.pending[slot] = []

    def flush(self):
        self.drain(0)
        self.drain(1)


def network(net, exchange, reducer):
    rows = net.rows
    top = net.top
    reducer_time = [0]

    def reduce_step():
        reducer.step(reducer_time[0])
        reducer_time[0] += 1

    hbm = net.hbm
    loads = {}
    for plane in range(4):
        loads["img", plane] = net.load(
            plane, hbm["image"].at[pl.ds(plane * rows, rows)], net.img.at[plane]
        )
    loads["wr"] = net.load(4, hbm["w_reduce"], net.wr)
    loads["gain"] = net.load(5, hbm["gain"], net.gain)
    loads["shift"] = net.load(6, hbm["shift"], net.shift)
    loads["ws"] = net.load(7, hbm["w_spatial"], net.wa)
    for k in range(2):
        for p in range(4):
            loads["short", 4 * k + p] = net.load(
                8 + 4 * k + p,
                hbm["w_short"].at[pl.ds(k * W, W), pl.ds(p * W, W)],
                net.wb.at[4 * k + p],
            )
    loads["we"] = net.load(16, hbm["w_expand"], net.we)
    loads["wr2"] = net.load(17, hbm["w_reduce2"], net.wr2)
    loads["we2"] = net.load(18, hbm["w_expand2"], net.we2)
    for p in range(4):
        loads["cot", p] = net.load(19 + p, hbm["cot"].at[:, pl.ds(p * W, W)], net.gh.at[p])
    net.entry()
    for plane in range(4):
        net.clear_margins(net.gz.at[plane])
    net.clear_margins(net.t4)

    loads["wr"].wait()
    msg = exchange.begin()
    results = None
    for plane in range(4):
        loads["img", plane].wait()
        net.f1[plane] = dot(net.img[plane], net.wr[...])
        new = net.measure(msg, None, net.f1.at[plane], False, net.h1.at[plane])
        results = new if results is None else jax.tree.map(jnp.add, results, new)
    net.put(msg, 0, results)
    exchange.start(1)
    side_sums = []

    def side(p):
        for k in range(2):
            loads["short", 4 * k + p].wait()
        net.f3[...] = dot(net.img[0, :, 0:W], net.wb[p]) + dot(net.img[0, :, W:], net.wb[4 + p])
        side_sums.append(net.measure(msg, None, net.f3, False, net.hs.at[p]))

    side(0)
    side(1)
    exchange.middle()
    side(2)
    side(3)
    exchange.last()
    total = exchange.finish()
    loads["gain"].wait()
    loads["shift"].wait()
    net.moments(total, 0, FIRST, 4)
    for plane in range(4):

        def keep_first(group, index, where, value, plane=plane):
            if group == 0:
                net.gz[plane, pl.ds(pl.multiple_of(index * BLK + BLK, BLK), BLK), :] = value
            else:
                there = pl.ds(pl.multiple_of((index - net.top_blocks) * BLK, BLK), BLK)
                net.nl[plane, there, :] = value.astype(jnp.bfloat16)

        net.activate(net.f1.at[plane], FIRST, keep_first)
    for tap in range(9):
        i, j = divmod(tap, 3)
        plane = 2 * (i != 1) + (j != 1)
        net.shifted(net.gz.at[plane], net.x.at[tap], -8 * (i == 0) - (j == 0))
        net.moved(net.nl.at[plane], 0, net.x.at[tap], -(i == 0), -(j == 0))
    save = pltpu.make_async_copy(net.x, hbm["x_keep"], net.load_sem.at[23])
    save.start()
    loads["ws"].wait()
    msg = exchange.begin()

    def conv(weights):
        total = dot(net.x[0], weights[0])
        for tap in range(1, 9):
            total = total + dot(net.x[tap], weights[tap])
        return total

    net.f3[...] = conv(net.wa)
    net.measure(msg, 0, net.f3, True, net.h2)
    loads["ws2"] = net.load(7, hbm["w_spatial2"], net.wa)
    exchange.start(1)
    exchange.middle()
    exchange.last()
    total = exchange.finish()
    net.moments(total, 0, SECOND)

    def plain(ref):
        def keep(group, index, where, value):
            ref[where, :] = value.astype(ref.dtype)

        return keep

    net.activate(net.f3, SECOND, plain(net.n2))
    loads["we"].wait()
    msg = exchange.begin()
    for p in range(4):
        net.f1[p] = dot(net.n2[...], net.we[:, p * W : (p + 1) * W])
        net.measure(msg, p, net.f1.at[p], False, net.h3.at[p])
        net.put(msg, 4 + p, side_sums[p])
    exchange.start(8)
    exchange.middle()
    exchange.last()
    total = exchange.finish()
    for p in range(8):
        net.moments(total, p, THIRD + p)

    def join(p, group):
        a3, b3 = net.affine(THIRD + p, group)
        a4, b4 = net.affine(SIDE + p, group)
        return a3, a4, b3 + b4

    for p in range(4):
        params = [join(p, group) for group in range(2)]

        def join_body(group, index, where, keep, carry, p=p, params=params):
            a3, a4, b = params[group]
            u = net.f1[p, where, :] * a3 + net.hs[p, where, :].astype(jnp.float32) * a4 + b
            net.o1[p, where, :] = keep(gelu(u)).astype(jnp.bfloat16)
            return carry

        net.sweep(join_body, 0)
    loads["wr2"].wait()
    msg = exchange.begin()
    value = dot(net.o1[0], net.wr2[0])
    for p in range(1, 4):
        value = value + dot(net.o1[p], net.wr2[p])
    net.f3[...] = value
    net.measure(msg, 0, net.f3, False, net.h4)
    exchange.start(1)
    exchange.middle()
    exchange.last()
    total = exchange.finish()
    net.moments(total, 0, FOURTH)

    def around(ref):
        def keep(group, index, where, value):
            if group == 0:
                net.t4[pl.ds(pl.multiple_of(index * BLK + BLK, BLK), BLK), :] = value
            ref[where, :] = value.astype(jnp.bfloat16)

        return keep

    net.activate(net.f3, FOURTH, around(net.small))
    save.wait()
    for tap in range(9):
        i, j = divmod(tap, 3)
        net.shifted(net.t4, net.x.at[tap], 8 * (i - 1) + j - 1)
        net.moved(net.small, top, net.x.at[tap], i - 1, j - 1)
    loads["ws2"].wait()
    msg = exchange.begin()
    net.f3[...] = conv(net.wa)
    net.measure(msg, 0, net.f3, True, net.h5)
    exchange.start(1)
    exchange.middle()
    exchange.last()
    total = exchange.finish()
    net.moments(total, 0, FIFTH)
    net.activate(net.f3, FIFTH, plain(net.n5))
    loads["we2"].wait()
    msg = exchange.begin()
    for p in range(4):
        net.f1[p] = dot(net.n5[...], net.we2[:, p * W : (p + 1) * W])
        net.measure(msg, p, net.f1.at[p], False)
    exchange.start(4)
    exchange.middle()
    exchange.last()
    total = exchange.finish()
    for p in range(4):
        net.moments(total, p, SIXTH + p)
        loads["cot", p].wait()
    msg = exchange.begin()
    outs = []
    for p in range(4):
        params = [
            net.affine(SIXTH + p, group) + net.standard(SIXTH + p, group) for group in range(2)
        ]

        def out_body(group, index, where, keep, carry, p=p, params=params):
            scale, offset, a, b = params[group]
            h = net.f1[p, where, :]
            u = h * scale + offset + net.o1[p, where, :].astype(jnp.float32)
            y, slope = gelu_both(u)
            grad = net.gh[p, where, :].astype(jnp.float32) * slope
            net.gh[p, where, :] = y.astype(jnp.bfloat16)
            net.gz[p, where, :] = grad
            first, cross = carry
            return first + net.fold(grad), cross + net.fold(grad * (h * a + b))

        net.put(msg, p, net.sweep(out_body, (net.zeros(), net.zeros())))
        out = pltpu.make_async_copy(
            net.gh.at[p], hbm["y"].at[:, pl.ds(p * W, W)], net.load_sem.at[p]
        )
        out.start()
        outs.append(out)
    exchange.start(4)
    exchange.middle()
    exchange.last()
    total = exchange.finish()
    for out in outs:
        out.wait()
    for p in range(4):
        net.back_sweep(
            SIXTH + p, total, p, net.gz.at[p], net.f1.at[p], plain(net.gh.at[p])
        )
    value = dot_t(net.gh[0], net.we2[:, 0:W])
    for p in range(1, 4):
        value = value + dot_t(net.gh[p], net.we2[:, p * W : (p + 1) * W])
    net.f3[...] = value
    msg = exchange.begin()
    net.through(msg, 0, FIFTH, net.f3, net.h5, False)
    exchange.start(1)
    for p in range(2):
        net.emit(0, 0, p * W, dot_rows(net.n5[...], net.gh[p]))
    exchange.middle()
    for p in range(2, 4):
        net.emit(0, 0, p * W, dot_rows(net.n5[...], net.gh[p]))
    net.flush()
    reduce_step()
    exchange.last()
    total = exchange.finish()
    net.back_sweep(FIFTH, total, 0, net.f3, net.h5, around(net.small))
    for p in range(8):
        loads["short", p] = None
    for tap in range(9):
        i, j = divmod(tap, 3)
        net.shifted(net.t4, net.wb.at[tap], 8 * (1 - i) + 1 - j)
        net.moved(net.small, top, net.wb.at[tap], 1 - i, 1 - j)
    where = pl.ds(0, rows)
    value = dot_t(net.wb[0, where, :], net.wa[0])
    for tap in range(1, 9):
        value = value + dot_t(net.wb[tap, where, :], net.wa[tap])
    net.f3[...] = value
    loads["ws"] = net.load(7, hbm["w_spatial"], net.wa)
    msg = exchange.begin()
    net.through(msg, 0, FOURTH, net.f3, net.h4, True)
    exchange.start(1)
    for tap in range(5):
        net.emit(1, tap * W, 0, dot_rows(net.x[tap], net.small[...]))
    exchange.middle()
    for tap in range(5, 9):
        net.emit(1, tap * W, 0, dot_rows(net.x[tap], net.small[...]))
    net.flush()
    reduce_step()
    loads["x"] = pltpu.make_async_copy(hbm["x_keep"], net.x, net.load_sem.at[23])
    loads["x"].start()
    exchange.last()
    total = exchange.finish()
    net.back_sweep(FOURTH, total, 0, net.f3, net.h4, plain(net.small))
    msg = exchange.begin()
    for p in range(4):
        net.gz[p] = net.gz[p] + dot_t(net.small[...], net.wr2[p])
        params = [
            join(p, group)
            + net.standard(THIRD + p, group)
            + net.standard(SIDE + p, group)
            for group in range(2)
        ]

        def join_back(group, index, where, keep, carry, p=p, params=params):
            a3, a4, b, sa3, sb3, sa4, sb4 = params[group]
            h3 = net.h3[p, where, :].astype(jnp.float32)
            hs = net.hs[p, where, :].astype(jnp.float32)
            slope = gelu_both(h3 * a3 + hs * a4 + b)[1]
            grad = net.gz[p, where, :] * slope
            net.gz[p, where, :] = grad
            first, cross3, cross4 = carry
            return (
                first + net.fold(grad),
                cross3 + net.fold(grad * (h3 * sa3 + sb3)),
                cross4 + net.fold(grad * (hs * sa4 + sb4)),
            )

        results = net.sweep(join_back, (net.zeros(), net.zeros(), net.zeros()))
        net.put(msg, p, results)
        net.put(msg, 4 + p, results, 1)
    exchange.start(8)
    for p in range(2):
        net.emit(2, p * W, 0, dot_rows(net.o1[p], net.small[...]))
    exchange.middle()
    for p in range(2, 4):
        net.emit(2, p * W, 0, dot_rows(net.o1[p], net.small[...]))
    exchange.last()
    net.flush()
    reduce_step()
    total = exchange.finish()
    for p in range(4):
        net.back_sweep(THIRD + p, total, p, net.gz.at[p], net.h3.at[p], plain(net.h3.at[p]))
        net.back_sweep(SIDE + p, total, 4 + p, net.gz.at[p], net.hs.at[p], plain(net.hs.at[p]))
    value = dot_t(net.h3[0], net.we[:, 0:W])
    for p in range(1, 4):
        value = value + dot_t(net.h3[p], net.we[:, p * W : (p + 1) * W])
    net.f3[...] = value
    msg = exchange.begin()
    net.through(msg, 0, SECOND, net.f3, net.h2, False)
    exchange.start(1)
    for p in range(4):
        net.emit(3, 0, p * W, dot_rows(net.n2[...], net.h3[p]))
    exchange.middle()
    for k in range(2):
        for p in range(4):
            net.emit(4, k * W, p * W, dot_rows(net.img[0, :, k * W : (k + 1) * W], net.hs[p]))
    exchange.last()
    net.flush()
    reduce_step()
    total = exchange.finish()
    net.back_sweep(SECOND, total, 0, net.f3, net.h2, around(net.small))
    for s in range(4):
        net.shifted(net.t4, net.wb.at[s], 8 * (s // 2) + s % 2)
        net.moved(net.small, top, net.wb.at[s], s // 2, s % 2)
    loads["ws"].wait()
    msg = exchange.begin()
    results = None
    for plane in range(4):
        value = None
        for tap in range(9):
            i, j = divmod(tap, 3)
            if 2 * (i != 1) + (j != 1) == plane:
                term = dot_t(net.wb[2 * (i == 0) + (j == 0), where, :], net.wa[tap])
                value = term if value is None else value + term
        net.f1[plane] = value
        new = net.through(msg, None, FIRST, net.f1.at[plane], net.h1.at[plane], True)
        results = new if results is None else jax.tree.map(jnp.add, results, new)
    net.put(msg, 0, results)
    for k in range(2):
        for p in range(4):
            loads["short", 4 * k + p] = net.load(
                8 + 4 * k + p,
                hbm["w_short"].at[pl.ds(k * W, W), pl.ds(p * W, W)],
                net.wb.at[4 * k + p],
            )
    exchange.start(1)
    loads["x"].wait()
    for tap in range(5):
        net.emit(5, tap * W, 0, dot_rows(net.x[tap], net.small[...]))
    exchange.middle()
    for tap in range(5, 9):
        net.emit(5, tap * W, 0, dot_rows(net.x[tap], net.small[...]))
    exchange.last()
    net.flush()
    reduce_step()
    total = exchange.finish()
    for plane in range(4):
        net.back_sweep(
            FIRST, total, 0, net.f1.at[plane], net.h1.at[plane], plain(net.h1.at[plane]), 4
        )
    for k in range(2):
        value = dot_rows(net.img[0, :, k * W : (k + 1) * W], net.h1[0])
        for plane in range(1, 4):
            value = value + dot_rows(net.img[plane, :, k * W : (k + 1) * W], net.h1[plane])
        net.emit(6, k * W, 0, value)
    net.flush()
    reduce_step()
    outs = []
    for plane in range(4):
        for k in range(2):
            value = dot_t(net.h1[plane], net.wr[k * W : (k + 1) * W, :])
            if plane == 0:
                for p in range(4):
                    if k == 0:
                        loads["short", p].wait()
                        loads["short", 4 + p].wait()
                    value = value + dot_t(net.hs[p], net.wb[4 * k + p])
            net.img[plane, :, k * W : (k + 1) * W] = value.astype(jnp.bfloat16)
        out = pltpu.make_async_copy(
            net.img.at[plane], hbm["grad_image"].at[pl.ds(plane * rows, rows)], net.load_sem.at[plane]
        )
        out.start()
        outs.append(out)
    while reducer_time[0] < reducer.groups + reducer.stages - 1:
        reduce_step()
    for out in outs:
        out.wait()


HBM_IN = (
    "image",
    "cot",
    "w_reduce",
    "w_spatial",
    "w_expand",
    "w_short",
    "w_reduce2",
    "w_spatial2",
    "w_expand2",
    "gain",
    "shift",
)
SHAPES = ((512, 2048), (4608, 512), (2048, 512), (512, 2048), (1024, 2048), (4608, 512), (1024, 512))


def whole_kernel(sizes, geometry, names, half, *refs):
    x_bits, dp_bits, _ = bit_counts(sizes)
    steps = x_bits + dp_bits
    place = [0]

    def some(number):
        start = place[0]
        place[0] += number
        return refs[start : place[0]]

    hbm = dict(zip(HBM_IN, some(len(HBM_IN))))
    hbm["y"], hbm["grad_image"] = some(2)
    outs = some(7)
    dgain, dshift = some(2)
    grads = some(7)
    (hbm["x_keep"],) = some(1)
    parts = dict(zip(names, some(len(names))))
    exchange = Exchange(sizes, some(7))
    lanes = len(axis_orders(sizes))
    rest = some(2 + lanes * steps + 6)
    landings = [rest[2 + steps * i : 2 + steps * (i + 1)] for i in range(lanes)]
    scratch = (rest[0], rest[1], landings) + tuple(rest[2 + lanes * steps :])
    reducer = Reducer(sizes, SHAPES, half, grads, outs, scratch)
    net = Net(sizes, geometry, parts)
    net.hbm, net.grads, net.dgain, net.dshift = hbm, grads, dgain, dshift

    def entry():
        semaphore = pltpu.get_barrier_semaphore()
        dp_size, grp_size = sizes
        for k in range(1, grp_size):
            pl.semaphore_signal(
                semaphore, inc=1, device_id=(reducer.dp, reducer.grp ^ k), device_id_type=MESH_ID
            )
        for k in range(1, dp_size):
            pl.semaphore_signal(
                semaphore, inc=1, device_id=(reducer.dp ^ k, reducer.grp), device_id_type=MESH_ID
            )
        pl.semaphore_wait(semaphore, dp_size + grp_size - 2)

    net.entry = entry
    network(net, exchange, reducer)


def run_network(image, cot, weights, gain, shift, crops, per):
    sizes = (lax.axis_size("dp"), lax.axis_size("grp"))
    dp_size, grp_size = sizes
    dp_bits = dp_size.bit_length() - 1
    half = 256 // dp_size
    rows = crops * 64 + 9 * per
    bf16, f32 = jnp.bfloat16, jnp.float32
    scratch = {
        "img": pltpu.VMEM((4, rows, 1024), bf16),
        "h1": pltpu.VMEM((4, rows, W), bf16),
        "x": pltpu.VMEM((9, rows, W), bf16),
        "f1": pltpu.VMEM((4, rows, W), f32),
        "h3": pltpu.VMEM((4, rows, W), bf16),
        "hs": pltpu.VMEM((4, rows, W), bf16),
        "o1": pltpu.VMEM((4, rows, W), bf16),
        "h2": pltpu.VMEM((rows, W), bf16),
        "h4": pltpu.VMEM((rows, W), bf16),
        "h5": pltpu.VMEM((rows, W), bf16),
        "n2": pltpu.VMEM((rows, W), bf16),
        "n5": pltpu.VMEM((rows, W), bf16),
        "small": pltpu.VMEM((rows, W), bf16),
        "gz": pltpu.VMEM((4, rows, W), f32),
        "gh": pltpu.VMEM((4, rows, W), bf16),
        "t4": pltpu.VMEM((crops * 64 + 2 * BLK, W), f32),
        "nl": pltpu.VMEM((4, 9 * per, W), bf16),
        "f3": pltpu.VMEM((rows, W), f32),
        "stage": pltpu.VMEM((2, W, W), f32),
        "wr": pltpu.VMEM((1024, W), bf16),
        "we": pltpu.VMEM((W, 2048), bf16),
        "wr2": pltpu.VMEM((4, W, W), bf16),
        "we2": pltpu.VMEM((W, 2048), bf16),
        "wa": pltpu.VMEM((9, W, W), bf16),
        "wb": pltpu.VMEM((9, W, W), bf16),
        "gain": pltpu.VMEM((16, 1, W), f32),
        "shift": pltpu.VMEM((16, 1, W), f32),
        "mom": pltpu.VMEM((16, 4, W), f32),
        "load_sem": pltpu.SemaphoreType.DMA((24,)),
        "stage_sem": pltpu.SemaphoreType.DMA((2, 32)),
    }
    own = 8 if 8 % grp_size else max(8 // grp_size, 4 if 4 % grp_size else 4 // grp_size)
    peers = max(sizes)
    exchange = [
        pltpu.VMEM((2, 8, 4, W), f32),
        pltpu.VMEM((2, grp_size, own, 4, W), f32),
        pltpu.VMEM((2, own, 4, W), f32),
        pltpu.VMEM((2, dp_size, own, 4, W), f32),
        pltpu.VMEM((2, 8, 4, W), f32),
        pltpu.SemaphoreType.DMA((2, 3, peers)),
        pltpu.SemaphoreType.DMA((2, 3, peers)),
    ]
    anywhere = pl.BlockSpec(memory_space=pl.ANY)
    inside = pl.BlockSpec(memory_space=pltpu.VMEM)
    shape = jax.ShapeDtypeStruct
    out_shape = (
        [shape((rows, 2048), bf16), shape((4 * rows, 1024), bf16)]
        + [shape((r // dp_size, c), f32) for r, c in SHAPES]
        + [shape((16, 1, W), f32)] * 2
        + [shape((2,) * dp_bits + (r // dp_size, c), f32) for r, c in SHAPES]
        + [shape((9, rows, W), bf16)]
    )
    return pl.pallas_call(
        functools.partial(whole_kernel, sizes, (crops, per), tuple(scratch), half),
        out_shape=out_shape,
        in_specs=[anywhere] * len(HBM_IN),
        out_specs=[anywhere] * 9 + [inside] * 2 + [anywhere] * 8,
        scratch_shapes=list(scratch.values()) + exchange + reducer_scratch(sizes, half),
        compiler_params=pltpu.CompilerParams(
            collective_id=1, has_side_effects=True, vmem_limit_bytes=VMEM_LIMIT
        ),
    )(image, cot, *weights, gain, shift)


VMEM_LIMIT = 64 * 2**20 - 2**16


def global_rows(value):
    crops, _, _, width = value.shape
    padded = jnp.pad(value, ((0, 0), (0, 1), (0, 1), (0, 0)))
    return padded.reshape(crops * 64, width)


def local_rows(value):
    return value.transpose(1, 2, 0, 3).reshape(-1, value.shape[3])


def global_back(value, crops):
    return value.reshape(crops, 8, 8, -1)[:, :7, :7]


def local_back(value, per):
    return value.reshape(3, 3, per, -1).transpose(2, 0, 1, 3)


def body(
    image_global,
    image_local,
    w_reduce,
    w_spatial,
    w_expand,
    w_short,
    w_reduce2,
    w_spatial2,
    w_expand2,
    gain_mid,
    shift_mid,
    gain_wide,
    shift_wide,
    cotangent_global,
    cotangent_local,
):
    crops, per = image_global.shape[0], image_local.shape[0]
    top = crops * 64
    rows = top + 9 * per
    planes = []
    for a in range(2):
        for b in range(2):
            planes.append(global_rows(image_global[:, a::2, b::2]))
            planes.append(local_rows(image_local[:, a::2, b::2]))
    image = jnp.concatenate(planes)
    cot = jnp.concatenate([global_rows(cotangent_global), local_rows(cotangent_local)])

    def pieces(mid, wide):
        parts = [mid[0:2], wide[0:2].reshape(8, W), mid[2:4], wide[2].reshape(4, W)]
        return jnp.concatenate(parts).reshape(16, 1, W)

    results = run_network(
        image,
        cot,
        [
            w_reduce,
            w_spatial.reshape(9, W, W),
            w_expand,
            w_short,
            w_reduce2.reshape(4, W, W),
            w_spatial2.reshape(9, W, W),
            w_expand2,
        ],
        pieces(gain_mid, gain_wide),
        pieces(shift_mid, shift_wide),
        crops,
        per,
    )
    y, grad_image = results[:2]
    expand2, spatial2, reduce2, expand, short, spatial, reduce = results[2:9]
    planes = grad_image.reshape(2, 2, rows, 1024)
    big = planes[:, :, :top].reshape(2, 2, crops, 8, 8, 1024)[:, :, :, :7, :7]
    big = big.transpose(2, 3, 0, 4, 1, 5).reshape(crops, 14, 14, 1024)
    little = planes[:, :, top:].reshape(2, 2, 3, 3, per, 1024)
    little = little.transpose(4, 2, 0, 3, 1, 5).reshape(per, 6, 6, 1024)

    def split(value):
        value = value.reshape(16, W)
        mid = jnp.concatenate([value[0:2], value[10:12]])
        wide = jnp.concatenate([value[2:10], value[12:16]]).reshape(3, 2048)
        return mid, wide

    gain_grads = split(results[9])
    shift_grads = split(results[10])
    return (
        global_back(y[:top], crops),
        local_back(y[top:], per),
        big,
        little,
        reduce,
        spatial,
        expand,
        short,
        reduce2,
        spatial2,
        expand2,
        gain_grads[0],
        shift_grads[0],
        gain_grads[1],
        shift_grads[1],
    )


def solution(mesh):
    crops = P(("dp", "grp"), None, None, None)
    in_specs = (crops, crops) + (P(),) * 11 + (crops, crops)
    out_specs = (crops,) * 4 + (P("dp", None),) * 7 + (P(),) * 4
    return jax.shard_map(body, mesh=mesh, in_specs=in_specs, out_specs=out_specs, check_vma=False)
```

time: 583 us -> 364 us (0.62); the launches traced: 572 us -> 360 us
  matrix products: 121 us -> 0 us
  other arithmetic: 64 us -> 2.52 us
  Pallas kernels: 345 us -> 318 us
    dot_general x30 -> x0, matrix products: 73.3 us -> none  [the longest x10 25.6 us: mix(): jnp.einsum('nhwc,cd->nhwd', value, weight, preferred_element_type=jnp.flo...]
    conv_general_dilated x12 -> x0, matrix products: 47.2 us -> none  [the longest x4 16 us: spatial_back(): lax.conv_general_dilated(grad, kernel, (1, 1), ((1, stride), (1, stride))...]
    pallas_call x13 -> x1, Pallas kernels: 345 us -> 318 us  [run_network(): pl.pallas_call(functools.partial(whole_kernel, sizes, (crops, per), tuple...]
    convert_element_type x17 -> x0, other arithmetic: 21.6 us -> none  [the longest x12 16.3 us: norm_back(): backs.append(value.astype(jnp.bfloat16))]
    pad x2 -> x5, local copies, waits for them, and re-layouts: 15.5 us -> 0.56 us  [global_rows(): padded = jnp.pad(value, ((0, 0), (0, 1), (0, 1), (0, 0)))]
    reduce_sum x5 -> x0, other arithmetic: 14.8 us -> none  [norm_back(): jnp.sum(item[0][group], axis=(0, 1, 2))]
    slice x5 -> x21, local copies, waits for them, and re-layouts: 3.03 us -> 12.7 us  [the longest x5 3.91 us: pieces(): parts = [mid[0:2], wide[0:2].reshape(8, W), mid[2:4], wide[2].reshape(4, W)]]
    add x6 -> x0, other arithmetic: 9.28 us -> none  [norm_back(): shift_grad = sums[0][start:start + width] + sums[2][start:start + width]]
where the time goes in v2:
time: 364 us; the launch traced here: 360 us
  Pallas kernels  318 us (87%)
  local copies, waits for them, and re-layouts  37.9 us (10%)
    pallas_call x1, Pallas kernels, run_network(): pl.pallas_call(functools.partial(whole_kernel, sizes, (crops, per), tuple...  318 us
    unnamed x49, local copies, waits for them, and re-layouts  18.7 us

profile of v2, /device:TPU:0, one launch (start us, length us, event | category | flops | bytes accessed | tf_op | source)
XLA Modules:
  0.0 359.7 jit_solution(844793654418454212)
XLA Ops:
  0.6 0.0 copy-start.6
  0.7 0.8 fusion.3
  1.4 0.8 fusion.2
  2.2 0.8 slice.123
  3.0 0.8 slice.127
  3.8 0.8 slice_reduce_fusion
  4.7 0.6 reshape.134.refs_10_
  5.3 0.6 reshape.132.refs_9_
  6.0 1.7 copy.52
  7.6 0.2 pad.21.clone
  7.8 0.0 copy-start.1
  7.8 0.0 copy-done.6
  7.9 1.3 pad_maximum_fusion.refs_1_
  9.1 0.0 copy-done.2
  9.1 0.1 fusion.1
  9.3 0.6 copy-done.1
  9.8 0.6 fusion
  10.4 0.1 copy.51
  10.6 0.1 pad.20.clone
  10.7 0.1 copy.49
  10.8 0.1 pad.18.clone
  10.9 0.1 copy.48
  11.0 0.1 pad.17.clone
  11.1 0.1 copy.50
  11.3 0.1 pad.19.clone
  11.4 0.8 constant_dynamic-update-slice_fusion.7
  12.2 0.7 constant_dynamic-update-slice_fusion.6
  13.0 0.9 constant_dynamic-update-slice_fusion.5
  13.8 0.7 constant_dynamic-update-slice_fusion.4
  14.6 0.8 constant_dynamic-update-slice_fusion.3
  15.4 0.7 constant_dynamic-update-slice_fusion.2
  16.1 0.9 constant_dynamic-update-slice_fusion.1
  17.0 0.7 constant_dynamic-update-slice_fusion.refs_0_
  17.7 318.2 %shard_map.262 = (bf16[400,2048]{1,0:T(8,128)(2,1)}, bf16[1600,1024]{1,0:T(8,128)(2,1)}, f32[64,2048]{1,0:T(8,128)}, f32[576,512]{1,0:T(8,128)}, f32[256,512]{1,...) custom-call(bf16[1600,1024]{1,0:T(8,128)(2,1)} %constant_dynamic-upd, ...), custom_call_target="tpu_custom_call" | custom-call | tf_op jit(solution)/shard_map/pallas_call | solution.py:1160
  335.9 0.7 slice.138
  336.6 0.7 slice.142
  337.3 0.7 slice.146
  338.0 0.7 slice.150
  338.7 0.7 slice.144
  339.4 0.8 copy.38
  340.2 0.6 pad_maximum_fusion.5
  340.8 0.6 reshape.142
  341.4 0.7 slice.148
  342.2 0.8 copy.39
  342.9 0.6 pad_maximum_fusion.6
  343.6 0.6 reshape.143
  344.2 2.1 slice.132
  346.3 1.3 slice.130
  347.6 0.1 slice.152
  347.6 1.6 copy.46
  349.2 0.0 copy-done
  349.2 0.1 slice.155
  349.3 0.2 slice.153
  349.5 0.2 slice.154
  349.7 0.0 copy-start.10
  349.7 2.6 copy.47
  352.3 1.1 copy.37
  353.4 0.7 copy.79
  354.1 1.0 copy.80
  355.1 0.8 copy.81
  355.9 1.0 copy.82
  356.9 0.8 copy.83
  357.7 1.0 copy.84
  358.7 0.8 copy.85
  (31 shorter events, 0.2 us)
Async XLA Ops:
  0.6 7.2 %copy-start.6 = (bf16[16,3,3,2048]{3,0,2,1:T(8,128)(2,1)S(1)}, bf16[16,3,3,2048]{3,0,2,1:T(8,128)(2,1)}, u32[]{:S(2)}) copy-start(bf16[16,3,3,2048]{3,0,2,1:T(8,128)(2,1)} %param.29) | copy-start | bytes 1769476
  6.0 3.2 copy-start.2
  7.8 2.0 copy-start.1
  344.2 5.0 %copy-start = (bf16[1600,1024]{1,0:T(8,128)(2,1)S(1)}, bf16[1600,1024]{1,0:T(8,128)(2,1)}, u32[]{:S(2)}) copy-start(bf16[1600,1024]{1,0:T(8,128)(2,1)} %get-tuple-element.27) | copy-start | bytes 9830404
  349.7 3.7 %copy-start.10 = (f32[128,512]{1,0:T(8,128)S(1)}, f32[128,512]{1,0:T(8,128)}, u32[]{:S(2)}) copy-start(f32[128,512]{1,0:T(8,128)} %get-tuple-element.70) | copy-start | bytes 786436
  349.7 4.4 %copy-start.4 = (f32[576,512]{1,0:T(8,128)S(1)}, f32[576,512]{1,0:T(8,128)}, u32[]{:S(2)}) copy-start(f32[576,512]{1,0:T(8,128)} %get-tuple-element.71) | copy-start | bytes 3538948
  352.3 2.8 copy-start.9
  352.3 3.6 %copy-start.5 = (f32[128,2048]{1,0:T(8,128)S(1)}, f32[128,2048]{1,0:T(8,128)}, u32[]{:S(2)}) copy-start(f32[128,2048]{1,0:T(8,128)} %get-tuple-element.73) | copy-start | bytes 3145732
  353.4 3.5 copy-start.8
  354.1 3.6 copy-start.3
  355.1 3.6 copy-start.7
